TPU v7x, 32 devices: a whole 2x2x4 slice. The times are simulated.
32 devices in a mesh: scan: 2 (over x), tile: 4 (over y, core), mode: 4 (over z).
Axes of the slice: x: 2, y: 2, z: 4, core: 2. Of those that a mesh axis runs over, the one named last changes fastest.
Arguments:
- object_field: float32 [8, 4, 16, 2, 384], P(None, 'tile'), may hold values from -6 to 6
- probe_modes: float32 [4, 256, 512], P('mode'), may hold values from -6 to 6
- intensities: float32 [8, 256, 256], P(('scan', 'tile')), may hold values from 0.1 to 4
- positions: int32 [8, 2], replicated, may hold values from 0 to 256, as said below
Outputs:
- new_object: float32 [8, 4, 16, 2, 384], P(None, 'tile')
- new_probe: float32 [4, 256, 512], P('mode')
Inputs may be any that keep to these rules, and one draw needn't show every extreme that they name: Row positions are multiples of 16; every window of 256 x 256 lies inside the object. Pattern 0 has the largest row and column corner, pattern 1 the corner (0, 0).
All inputs are finite; a program needn't handle non-finite values.
Results may differ from a plain program's by a relative error of at most 0.0003.
Values sent between devices are 32-bit elements; how exact they have to be, the bound alone decides.
A program may use at most 64 MiB of HBM per device.

v0:
```python
import math

import jax
import jax.numpy as jnp
from jax import lax
from jax.sharding import PartitionSpec as P

floor_level = 0.1
damping = 1.0
highest = lax.Precision.HIGHEST


def transform_tables(width):
    index = jnp.arange(width, dtype=jnp.int32)
    phase = (index[:, None] * index[None, :] % width).astype(jnp.float32)
    angle = phase * (2.0 * math.pi / width)
    cosine = jnp.cos(angle) / math.sqrt(width)
    sine = -jnp.sin(angle) / math.sqrt(width)
    forward_rows = jnp.block([[cosine, sine], [-sine, cosine]])
    inverse_rows = jnp.block([[cosine, -sine], [sine, cosine]])
    return (cosine, sine, forward_rows, inverse_rows)


def times(left, right):
    half = left.shape[-1] // 2
    return jnp.concatenate(
        [
            left[..., :half] * right[..., :half] - left[..., half:] * right[..., half:],
            left[..., :half] * right[..., half:] + left[..., half:] * right[..., :half],
        ],
        -1,
    )


def conj_times(left, right):
    half = left.shape[-1] // 2
    return jnp.concatenate(
        [
            left[..., :half] * right[..., :half] + left[..., half:] * right[..., half:],
            left[..., :half] * right[..., half:] - left[..., half:] * right[..., :half],
        ],
        -1,
    )


def power(values):
    half = values.shape[-1] // 2
    return values[..., :half] ** 2 + values[..., half:] ** 2


def columns_forward(cosine, sine, data):
    half = data.shape[-1] // 2
    first = jnp.einsum("ab,pbc->pac", cosine, data, precision=highest)
    second = jnp.einsum("ab,pbc->pac", sine, data, precision=highest)
    return jnp.concatenate(
        [first[..., :half] - second[..., half:], first[..., half:] + second[..., :half]], -1
    )


def columns_inverse(cosine, sine, data):
    half = data.shape[-1] // 2
    first = jnp.einsum("ab,pbc->pac", cosine, data, precision=highest)
    second = jnp.einsum("ab,pbc->pac", sine, data, precision=highest)
    return jnp.concatenate(
        [first[..., :half] + second[..., half:], first[..., half:] - second[..., :half]], -1
    )


def project(cosine, sine, spectra, intensities):
    far_field = columns_forward(cosine, sine, spectra)
    total_power = lax.psum(power(far_field), "mode")
    ratio_map = jnp.sqrt(intensities / jnp.maximum(total_power, floor_level))
    return columns_inverse(cosine, sine, far_field * jnp.concatenate([ratio_map, ratio_map], -1))


def pick_rows(rows, picks):
    return rows[picks]


def assemble(received, order):
    moved = jnp.swapaxes(received, 0, 1)
    picked = jax.vmap(pick_rows)(moved, order)
    ordered = jnp.swapaxes(picked, 1, 2)
    return ordered.reshape(ordered.shape[0], -1, ordered.shape[-1])


def disassemble(ordered, order):
    moved = jnp.swapaxes(ordered, 1, 2)
    picked = jax.vmap(pick_rows)(moved, order)
    return jnp.swapaxes(picked, 0, 1)


def place(cycle_flat, col_flat, terms, weights, shape):
    cycle_count, block, columns = shape
    count, rows, doubled = terms.shape
    width = doubled // 2
    span = jnp.arange(width, dtype=jnp.int32)
    split_terms = terms.reshape(count, rows, 2, width)
    numerator = jnp.zeros((cycle_count, block, 2, columns), jnp.float32)
    numerator = numerator.at[
        cycle_flat[:, None, None, None],
        jnp.arange(rows, dtype=jnp.int32)[None, :, None, None],
        jnp.arange(2, dtype=jnp.int32)[None, None, :, None],
        col_flat[:, None, None, None] + span,
    ].add(split_terms)
    weight = jnp.zeros((cycle_count, block, columns), jnp.float32)
    weight = weight.at[
        cycle_flat[:, None, None],
        jnp.arange(block, dtype=jnp.int32)[None, :, None],
        col_flat[:, None, None] + span,
    ].add(weights)
    return (numerator, weight)


def on_device(object_field, probe_modes, intensities, positions):
    width = probe_modes.shape[1]
    cycles = object_field.shape[0]
    block = object_field.shape[2]
    columns = object_field.shape[4]
    tiles = lax.axis_size("tile")
    patterns = intensities.shape[0]
    blocks = width // block
    rounds = blocks // tiles
    scan_index = lax.axis_index("scan")
    tile_index = lax.axis_index("tile")
    group = lax.dynamic_slice_in_dim(
        positions, scan_index * (tiles * patterns), tiles * patterns, 0
    )
    group = group.reshape(tiles, patterns, 2)
    start_blocks = group[:, :, 0] // block
    start_cols = group[:, :, 1]
    own_starts = lax.dynamic_index_in_dim(start_blocks, tile_index, 0, keepdims=False)
    first_block = jnp.mod(tile_index - start_blocks, tiles)
    patch_blocks = first_block[:, :, None] + tiles * jnp.arange(rounds, dtype=jnp.int32)
    cycle_flat = ((start_blocks[:, :, None] + patch_blocks) // tiles).reshape(-1)
    col_flat = jnp.broadcast_to(start_cols[:, :, None], patch_blocks.shape).reshape(-1)
    patch_flat = patch_blocks.reshape(-1)
    count = patch_flat.shape[0]
    lanes = jnp.arange(tiles, dtype=jnp.int32)
    gather_order = jnp.mod(lanes[None, :] + own_starts[:, None], tiles)
    scatter_order = jnp.mod(lanes[None, :] - own_starts[:, None], tiles)
    cosine, sine, forward_rows, inverse_rows = transform_tables(width)
    selector = (patch_flat[None, :] == jnp.arange(blocks, dtype=jnp.int32)[:, None]).astype(
        jnp.float32
    )
    current = object_field[:, 0]
    probe_now = probe_modes[0]

    def cut(cycle, column):
        piece = lax.dynamic_slice(current, (cycle, 0, 0, column), (1, block, 2, width))
        return piece.reshape(block, 2 * width)

    object_rows = jax.vmap(cut)(cycle_flat, col_flat)
    probe_rows = probe_now.reshape(blocks, block, 2 * width)[patch_flat]
    exit_rows = times(probe_rows, object_rows)
    spectra = jnp.dot(exit_rows.reshape(-1, 2 * width), forward_rows, precision=highest)
    arrived = lax.all_to_all(
        spectra.reshape(tiles, patterns, rounds, block, 2 * width),
        "tile",
        split_axis=0,
        concat_axis=0,
        tiled=True,
    )
    returned = project(cosine, sine, assemble(arrived, gather_order), intensities)
    outgoing = disassemble(
        returned.reshape(patterns, rounds, tiles, block, 2 * width), scatter_order
    )
    came_back = lax.all_to_all(outgoing, "tile", split_axis=0, concat_axis=0, tiled=True)
    new_rows = jnp.dot(came_back.reshape(-1, 2 * width), inverse_rows, precision=highest)
    difference = new_rows.reshape(count, block, 2 * width) - exit_rows
    terms = conj_times(probe_rows, difference)
    mixed = jnp.concatenate([conj_times(object_rows, difference), power(object_rows)], -1)
    probe_stats = jnp.dot(selector, mixed.reshape(count, -1), precision=highest).reshape(
        width, 3 * width
    )
    numerator, weight = place(
        cycle_flat, col_flat, terms, power(probe_rows), (cycles, block, columns)
    )
    numerator, weight = lax.psum((numerator, weight), ("scan", "mode"))
    summed = lax.psum(probe_stats, ("scan", "tile"))
    divisor = summed[:, 2 * width :]
    probe_next = probe_now + summed[:, : 2 * width] / jnp.concatenate([divisor, divisor], -1)
    current = current + numerator / (weight[:, :, None, :] + damping)
    return (current[:, None], probe_next[None])


def solution(mesh):
    in_specs = (
        P(None, "tile", None, None, None),
        P("mode", None, None),
        P(("scan", "tile"), None, None),
        P(),
    )
    out_specs = (P(None, "tile", None, None, None), P("mode", None, None))
    return jax.shard_map(
        on_device, mesh=mesh, in_specs=in_specs, out_specs=out_specs, check_vma=False
    )
```

profile of v0, /device:TPU:0, one launch (start us, length us, event | category | flops | bytes accessed | tf_op | source)
XLA Modules:
  0.0 1655.2 jit_solution(11159671763615277630)
XLA Ops:
  11.3 4.0 copy.52
  15.2 7.7 gather_fusion.1
  22.9 6.3 copy.54
  29.2 2.3 reshape.658
  31.5 2.4 gather_fusion
  36.0 3.1 convolution_bitcast_fusion.4
  39.1 4.2 all-to-all-start
  46.3 6.5 all-to-all-done
  52.8 2.4 gather_fusion.2
  62.7 34.7 %all-reduce.5.cloned.1.call-done = f32[1,256,256]{1,2,0:T(8,128)} async-done(((f32[1,256,256]{1,2,0:T(8,128)}), f32[1,256,256]{1,2,0:T(8,128)}) %all-reduce.5.cloned.1.call-update) | async-done | bytes 262160 | tf_op jit(solution)/shard_map/psum | solution.py:71
  98.7 2.6 convolution_bitcast_fusion
  103.8 2.1 copy.58
  107.7 2.4 gather_fusion.3
  110.1 4.3 all-to-all-start.1
  118.7 4.7 all-to-all-done.1
  123.3 2.7 convolution_subtract_fusion
  128.9 2.2 reshape.664
  136.6 452.2 %scatter_custom_fusion.1 = f32[49152]{0:T(1024)S(1)} fusion(s32[65536]{0:T(1024)} %bitcast.129, f32[65536]{0:T(1024)} %bitcast.130, f32[]{:T(128)} %constant.104.clone.1), kind=kCustom, calls=%fused_computation.75 | custom fusion | flops 65536 | bytes 197120
  591.5 903.6 %scatter_custom_fusion = f32[98304]{0:T(1024)S(1)} fusion(s32[131072]{0:T(1024)} %bitcast.124, f32[131072]{0:T(1024)} %bitcast.125, f32[]{:T(128)} %constant.104.clone.1), kind=kCustom, calls=%fused_computation.71 | custom fusion | flops 131072 | bytes 393728
  1496.2 5.0 copy.61
  1502.1 2.1 fusion.18
  1504.3 130.5 %all-reduce.9.cloned.1.call-done = (f32[8,16,2,384]{1,2,0,3:T(2,128)}, f32[8,16,384]{2,1,0:T(8,128)}) async-done(((f32[8,16,2,384]{1,2,0,3:T(2,128)}, f32[8,16,384]{2,1,0:T(8,128)}), (f32[8,16,2,384]{1,2,0,3:T(2,128)}, f32[8,16,384]{2,1,0:T(8,128)})) %all-reduce.9.cloned.1.call-update) | async-done | bytes 589840 | tf_op jit(solution)/shard_map/psum | solution.py:179
  1637.4 6.3 fusion
  1643.6 5.0 copy.63
  (104 shorter events, 41.9 us)
Async XLA Ops:
  7.2 3.5 copy-start
  35.2 0.7 copy-start.7
  35.2 0.8 copy-start.8
  36.0 9.2 copy-start.14
  36.0 10.1 copy-start.13
  39.1 13.7 all-to-all-start
  43.3 54.2 %all-reduce.5.cloned.1.call-start = ((), (), s32[]{:S(2)}) async-start(), calls=%async_computation.2 | async-start | bytes 524288 | tf_op jit(solution)/shard_map/psum | solution.py:71
  97.5 3.8 copy-start.10
  97.5 3.8 copy-start.11
  110.1 8.0 copy-start.12
  110.1 13.2 all-to-all-start.1
  114.4 1386.8 %all-reduce.7.cloned.1.call-start = ((), (), s32[]{:S(2)}) async-start(), calls=%async_computation.3 | async-start | bytes 1572864 | tf_op jit(solution)/shard_map/psum | solution.py:180
  116.2 0.8 copy-start.2
  116.3 0.9 copy-start.3
  116.4 1.0 copy-start.4
  117.4 0.8 copy-start.5
  123.3 2.7 copy-start.1
  123.3 2.7 copy-start.6
  127.5 3.8 copy-start.15
  131.1 1503.7 %all-reduce.9.cloned.1.call-start = ((), (), s32[]{:S(2)}) async-start(), calls=%async_computation.4 | async-start | bytes 6684672 | tf_op jit(solution)/shard_map/psum | solution.py:179
  131.4 1.9 copy-start.9
Sparse Core Ops, SparseCore 0:
  61.0 36.4 all-reduce.4
  131.2 54.3 all-reduce.6
  1501.3 133.4 all-reduce.8
where the time goes:
time: 1660 us
  other arithmetic  1380 us (83%)
  waiting for transfers between devices  176 us (11%)
  local copies, waits for them, and re-layouts  59.4 us (4%)
    unnamed x8, other arithmetic  1360 us
    psum x1, waiting for transfers between devices, on_device(): numerator, weight = lax.psum((numerator, weight), ('scan', 'mode'))  131 us
    psum x1, waiting for transfers between devices, project(): total_power = lax.psum(power(far_field), 'mode')  34.7 us
  transfers between devices with their start and end apart: 5, of which 4 were waited for; matrix products, arithmetic and copies ran while one was open for 83% of the time, Pallas kernels for 0%

commit v1 on v0

--- a/solution.py
+++ b/solution.py
@@ -1,8 +1,13 @@
+import functools
 import math
 
 import jax
 import jax.numpy as jnp
+import ml_dtypes
+import numpy as np
 from jax import lax
+from jax.experimental import pallas as pl
+from jax.experimental.pallas import tpu as pltpu
 from jax.sharding import PartitionSpec as P
 
 floor_level = 0.1
@@ -184,6 +189,416 @@
     return (current[:, None], probe_next[None])
 
 
+MESH = pl.DeviceIdType.MESH
+VMEM = pl.BlockSpec(memory_space=pltpu.VMEM)
+SMEM = pl.BlockSpec(memory_space=pltpu.SMEM)
+vmem_bytes = 40 * 1024 * 1024
+f32 = jnp.float32
+
+
+def split_tables(width):
+    index = np.arange(width)
+    angle = (index[:, None] * index[None, :] % width) * (2.0 * math.pi / width)
+    cosine = np.cos(angle) / math.sqrt(width)
+    sine = -np.sin(angle) / math.sqrt(width)
+    right = np.block([[cosine, sine], [-sine, cosine]])
+    parts = []
+    for table in (right, right.T):
+        high = table.astype(ml_dtypes.bfloat16)
+        low = (table - high.astype(np.float64)).astype(ml_dtypes.bfloat16)
+        parts += [high, low]
+    return parts
+
+
+def halves(values):
+    high = values.astype(jnp.bfloat16)
+    return high, (values - high.astype(f32)).astype(jnp.bfloat16)
+
+
+def dot(left, right):
+    return jnp.dot(left, right, preferred_element_type=f32)
+
+
+def right_product(values, high_table, low_table):
+    high, low = halves(values)
+    return dot(high, high_table) + (dot(low, high_table) + dot(high, low_table))
+
+
+def left_product(high_table, low_table, values):
+    half = values.shape[-1] // 2
+    high, low = halves(jnp.concatenate([values[:, :half], values[:, half:]], 0))
+    out = dot(high_table, high) + (dot(high_table, low) + dot(low_table, high))
+    rows = out.shape[0] // 2
+    return jnp.concatenate([out[:rows], out[rows:]], 1)
+
+
+def sends(me, count, id_of, src_of, dst, send, recv):
+    copies = []
+    for step in range(1, count):
+        peer = lax.rem(me + step, count)
+        copies.append(
+            pltpu.make_async_remote_copy(
+                src_ref=src_of(peer),
+                dst_ref=dst.at[me],
+                send_sem=send.at[step - 1],
+                recv_sem=recv.at[step - 1],
+                device_id=id_of(peer),
+                device_id_type=MESH,
+            )
+        )
+    for copy in copies:
+        copy.start()
+    return copies
+
+
+def greet(groups):
+    barrier = pltpu.get_barrier_semaphore()
+    total = 0
+    for me, count, id_of in groups:
+        for step in range(1, count):
+            pl.semaphore_signal(
+                barrier, inc=1, device_id=id_of(lax.rem(me + step, count)), device_id_type=MESH
+            )
+            total += 1
+    pl.semaphore_wait(barrier, total)
+
+
+def tile_id(peer):
+    return {"tile": peer}
+
+
+def mode_id(peer):
+    return {"mode": peer}
+
+
+def pattern_id(tiles, peer):
+    return {"scan": peer // tiles, "tile": lax.rem(peer, tiles)}
+
+
+def any_id(tiles, modes, peer):
+    return {
+        "scan": peer // (tiles * modes),
+        "tile": lax.rem(peer // modes, tiles),
+        "mode": lax.rem(peer, modes),
+    }
+
+
+def fetch_kernel(sizes, rows_ref, square_ref, got_ref, squares_ref, send, recv, send_p, recv_p):
+    scans, tiles, modes = sizes
+    tile, mode = lax.axis_index("tile"), lax.axis_index("mode")
+    greet([(tile, tiles, tile_id), (mode, modes, mode_id)])
+    copies = sends(tile, tiles, tile_id, lambda peer: rows_ref.at[peer], got_ref, send, recv)
+    copies += sends(mode, modes, mode_id, lambda peer: square_ref, squares_ref, send_p, recv_p)
+    got_ref[tile] = rows_ref[tile]
+    squares_ref[mode] = square_ref[...]
+    for copy in copies:
+        copy.wait()
+
+
+def forward_kernel(
+    tiles, place_ref, got_ref, squares_ref, probe_ref, rh, rl, gh, gl,
+    window_ref, far_ref, power_ref, square_ref,
+):
+    width = probe_ref.shape[0]
+    block = got_ref.shape[3]
+    columns = got_ref.shape[4]
+    start, col = place_ref[0], place_ref[1]
+    shift = lax.rem(columns - col, columns)
+    for index in range(width // block):
+        owner = lax.rem(start + index, tiles)
+        for part in range(2):
+            piece = got_ref[owner, index // tiles, part]
+            window_ref[index * block : (index + 1) * block, part * width : (part + 1) * width] = (
+                pltpu.roll(piece, shift, 1)[:, :width]
+            )
+    waves = times(probe_ref[...], window_ref[...])
+    far = left_product(gh[...], gl[...], right_product(waves, rh[...], rl[...]))
+    far_ref[...] = far
+    power_ref[...] = power(far)
+    square_ref[...] = jnp.sum(squares_ref[...], axis=0)
+
+
+def ratio_kernel(
+    sizes, power_ref, square_ref, measured_ref, ratio_ref, squares_ref,
+    got, send, recv, send_r, recv_r, send_p, recv_p,
+):
+    scans, tiles, modes = sizes
+    mode = lax.axis_index("mode")
+    me = lax.axis_index("scan") * tiles + lax.axis_index("tile")
+    id_of = functools.partial(pattern_id, tiles)
+    greet([(mode, modes, mode_id), (me, scans * tiles, id_of)])
+    first = sends(mode, modes, mode_id, lambda peer: power_ref.at[peer], got, send, recv)
+    other = sends(me, scans * tiles, id_of, lambda peer: square_ref, squares_ref, send_p, recv_p)
+    got[mode] = power_ref[mode]
+    squares_ref[me] = square_ref[...]
+    for copy in first:
+        copy.wait()
+    total = got[0]
+    for index in range(1, modes):
+        total = total + got[index]
+    ratio_ref[mode] = jnp.sqrt(measured_ref[mode] / jnp.maximum(total, floor_level))
+    last = sends(
+        mode, modes, mode_id, lambda peer: ratio_ref.at[mode], ratio_ref, send_r, recv_r
+    )
+    for copy in last + other:
+        copy.wait()
+
+
+def inverse_kernel(
+    tiles, place_ref, ratio_ref, far_ref, window_ref, probe_ref, rh, rl, gh, gl,
+    terms_ref, mixed_ref,
+):
+    width = probe_ref.shape[0]
+    block = terms_ref.shape[2]
+    start = place_ref[0]
+    ratio = ratio_ref[...]
+    scaled = far_ref[...] * jnp.concatenate([ratio, ratio], 1)
+    waves = left_product(rh[...], rl[...], right_product(scaled, gh[...], gl[...]))
+    probe, window = probe_ref[...], window_ref[...]
+    difference = waves - times(probe, window)
+    terms = conj_times(probe, difference)
+    for index in range(width // block):
+        owner = lax.rem(start + index, tiles)
+        terms_ref[owner, index // tiles] = terms[index * block : (index + 1) * block]
+    mixed_ref[...] = jnp.concatenate([conj_times(window, difference), power(window)], 1)
+
+
+def reduce_kernel(
+    sizes, terms_ref, mixed_ref, probe_ref, all_ref, next_ref,
+    got, got_p, summed,
+    send, recv, send_m, recv_m, send_b, recv_b, send_n, recv_n,
+):
+    scans, tiles, modes = sizes
+    width2 = probe_ref.shape[-1]
+    count = scans * tiles
+    scan, tile, mode = lax.axis_index("scan"), lax.axis_index("tile"), lax.axis_index("mode")
+    me = scan * tiles + tile
+    id_of = functools.partial(pattern_id, tiles)
+    greet([(me * modes + mode, count * modes, functools.partial(any_id, tiles, modes))])
+    first = sends(mode, modes, mode_id, lambda peer: terms_ref.at[peer], got, send, recv)
+    second = sends(me, count, id_of, lambda peer: mixed_ref.at[peer], got_p, send_m, recv_m)
+    got[mode] = terms_ref[mode]
+    got_p[me] = mixed_ref[me]
+    for copy in first:
+        copy.wait()
+    total = got[0]
+    for index in range(1, modes):
+        total = total + got[index]
+    summed[...] = total
+    mine = tile == mode
+    copies = []
+    for scan_step in range(scans):
+        for mode_step in range(modes):
+            slot = scan_step * modes + mode_step
+            copy = pltpu.make_async_remote_copy(
+                src_ref=summed,
+                dst_ref=all_ref.at[me],
+                send_sem=send_b.at[slot],
+                recv_sem=recv_b.at[me],
+                device_id={
+                    "scan": lax.rem(scan + scan_step, scans),
+                    "tile": mode,
+                    "mode": lax.rem(mode + mode_step, modes),
+                },
+                device_id_type=MESH,
+            )
+            copies.append(copy)
+            if slot == 0:
+                pl.when(jnp.logical_not(mine))(copy.start)
+            else:
+                copy.start()
+
+    @pl.when(mine)
+    def _():
+        all_ref[me] = summed[...]
+
+    for copy in second:
+        copy.wait()
+    totals = got_p[0]
+    for index in range(1, count):
+        totals = totals + got_p[index]
+    divisor = totals[:, width2:]
+    next_ref[me] = probe_ref[me] + totals[:, :width2] / jnp.concatenate([divisor, divisor], 1)
+    last = sends(me, count, id_of, lambda peer: next_ref.at[me], next_ref, send_n, recv_n)
+    for slot, copy in enumerate(copies):
+        if slot == 0:
+            pl.when(jnp.logical_not(mine))(copy.wait_send)
+        else:
+            copy.wait_send()
+    for source in range(count):
+
+        def arrived(source=source):
+            pltpu.make_async_remote_copy(
+                src_ref=summed,
+                dst_ref=all_ref.at[source],
+                send_sem=send_b.at[0],
+                recv_sem=recv_b.at[source],
+                device_id={"mode": mode},
+                device_id_type=MESH,
+            ).wait_recv()
+
+        pl.when(jnp.logical_not(jnp.logical_and(mine, me == source)))(arrived)
+    for copy in last:
+        copy.wait()
+
+
+def update_kernel(tiles, places_ref, all_ref, square_ref, object_ref, out_ref, weight):
+    count, rounds, block, width2 = all_ref.shape
+    width = width2 // 2
+    columns = object_ref.shape[-1]
+    tile = places_ref[count, 0]
+    out_ref[...] = jnp.zeros_like(out_ref)
+    weight[...] = jnp.zeros_like(weight)
+    blank = jnp.zeros((block, columns - width), f32)
+
+    def add(pattern, carry):
+        start, col = places_ref[pattern, 0], places_ref[pattern, 1]
+        offset = lax.rem(tile - start + tiles * block * block, tiles)
+        cycle = (start + offset) // tiles
+        for index in range(rounds):
+            for part in range(2):
+                piece = all_ref[pattern, index, :, part * width : (part + 1) * width]
+                out_ref[cycle + index, part] += pltpu.roll(
+                    jnp.concatenate([piece, blank], 1), col, 1
+                )
+            weight[cycle + index] += pltpu.roll(
+                jnp.concatenate([square_ref[offset + tiles * index], blank], 1), col, 1
+            )
+        return carry
+
+    lax.fori_loop(0, count, add, 0)
+    divisor = weight[...] + damping
+    for part in range(2):
+        out_ref[:, part] = object_ref[:, part] + out_ref[:, part] / divisor
+
+
+def shape(*dims):
+    return jax.ShapeDtypeStruct(dims, f32)
+
+
+def dma(count):
+    return pltpu.SemaphoreType.DMA((count,))
+
+
+def local(kernel, in_specs, outs, scratch=()):
+    return pl.pallas_call(
+        kernel,
+        out_shape=outs,
+        in_specs=in_specs,
+        out_specs=jax.tree.map(lambda _: VMEM, outs),
+        scratch_shapes=list(scratch),
+        compiler_params=pltpu.CompilerParams(vmem_limit_bytes=vmem_bytes),
+    )
+
+
+def remote(kernel, number, inputs, outs, scratch):
+    return pl.pallas_call(
+        kernel,
+        out_shape=outs,
+        in_specs=[VMEM] * inputs,
+        out_specs=[VMEM] * len(outs),
+        scratch_shapes=scratch,
+        compiler_params=pltpu.CompilerParams(
+            collective_id=number, has_side_effects=True, vmem_limit_bytes=vmem_bytes
+        ),
+    )
+
+
+def one_wave(sizes, tables, object_field, probe_modes, intensities, positions):
+    scans, tiles, modes = sizes
+    count = scans * tiles
+    width = probe_modes.shape[1]
+    cycles, _, block, _, columns = object_field.shape
+    blocks = width // block
+    rounds = blocks // tiles
+    share = width // count
+    quarter = width // modes
+    scan, tile = lax.axis_index("scan"), lax.axis_index("tile")
+    me = scan * tiles + tile
+    starts = positions[:, 0] // block
+    places = jnp.stack([starts, positions[:, 1]], 1)
+    place_now = lax.dynamic_index_in_dim(places, me, 0, keepdims=False)
+    probe = probe_modes[0]
+    planar = jnp.swapaxes(object_field[:, 0], 1, 2)
+    group = lax.dynamic_slice_in_dim(starts, scan * tiles, tiles, 0)
+    first_cycle = (group + jnp.mod(tile - group, tiles)) // tiles
+    rows = jnp.stack(
+        [
+            lax.dynamic_slice_in_dim(planar, first_cycle[index], rounds, 0)
+            for index in range(tiles)
+        ]
+    )
+    square = power(lax.dynamic_slice_in_dim(probe, me * share, share, 0))
+    got, squares = remote(
+        functools.partial(fetch_kernel, sizes),
+        0,
+        2,
+        [shape(tiles, rounds, 2, block, columns), shape(modes, share, width)],
+        [dma(tiles - 1), dma(tiles - 1), dma(modes - 1), dma(modes - 1)],
+    )(rows, square)
+    window, far, strength, square = local(
+        functools.partial(forward_kernel, tiles),
+        [SMEM] + [VMEM] * 7,
+        [
+            shape(width, 2 * width),
+            shape(width, 2 * width),
+            shape(width, width),
+            shape(share, width),
+        ],
+    )(place_now, got, squares, probe, *tables)
+    ratio, squares = remote(
+        functools.partial(ratio_kernel, sizes),
+        1,
+        3,
+        [shape(modes, quarter, width), shape(count, share, width)],
+        [pltpu.VMEM((modes, quarter, width), f32)]
+        + [dma(modes - 1)] * 4
+        + [dma(count - 1)] * 2,
+    )(
+        strength.reshape(modes, quarter, width),
+        square,
+        intensities.reshape(modes, quarter, width),
+    )
+    terms, mixed = local(
+        functools.partial(inverse_kernel, tiles),
+        [SMEM] + [VMEM] * 8,
+        [shape(tiles, rounds, block, 2 * width), shape(width, 3 * width)],
+    )(place_now, ratio.reshape(width, width), far, window, probe, *tables)
+    everything, probe_next = remote(
+        functools.partial(reduce_kernel, sizes),
+        2,
+        3,
+        [shape(count, rounds, block, 2 * width), shape(count, share, 2 * width)],
+        [
+            pltpu.VMEM((modes, rounds, block, 2 * width), f32),
+            pltpu.VMEM((count, share, 3 * width), f32),
+            pltpu.VMEM((rounds, block, 2 * width), f32),
+        ]
+        + [dma(modes - 1)] * 2
+        + [dma(count - 1)] * 2
+        + [dma(scans * modes), dma(count)]
+        + [dma(count - 1)] * 2,
+    )(
+        terms,
+        mixed.reshape(count, share, 3 * width),
+        probe.reshape(count, share, 2 * width),
+    )
+    own = jnp.stack([tile, tile])[None].astype(jnp.int32)
+    updated = local(
+        functools.partial(update_kernel, tiles),
+        [SMEM] + [VMEM] * 3,
+        shape(cycles, 2, block, columns),
+        [pltpu.VMEM((cycles, block, columns), f32)],
+    )(
+        jnp.concatenate([places, own], 0),
+        everything,
+        squares.reshape(blocks, block, width),
+        planar,
+    )
+    new_object = jnp.swapaxes(updated, 1, 2)[:, None]
+    return (new_object, probe_next.reshape(1, width, 2 * width))
+
+
 def solution(mesh):
     in_specs = (
         P(None, "tile", None, None, None),
@@ -192,6 +607,19 @@
         P(),
     )
     out_specs = (P(None, "tile", None, None, None), P("mode", None, None))
-    return jax.shard_map(
-        on_device, mesh=mesh, in_specs=in_specs, out_specs=out_specs, check_vma=False
-    )
+    sizes = (mesh.shape["scan"], mesh.shape["tile"], mesh.shape["mode"])
+
+    def run(object_field, probe_modes, intensities, positions):
+        body = on_device
+        if (
+            sizes[1] == sizes[2]
+            and probe_modes.shape[0] == sizes[2]
+            and intensities.shape[0] == sizes[0] * sizes[1]
+        ):
+            tables = [jnp.asarray(table) for table in split_tables(probe_modes.shape[1])]
+            body = functools.partial(one_wave, sizes, tables)
+        return jax.shard_map(
+            body, mesh=mesh, in_specs=in_specs, out_specs=out_specs, check_vma=False
+        )(object_field, probe_modes, intensities, positions)
+
+    return run

time: 1660 us -> 96.2 us (0.06)
  the two profiles are of different devices: /device:TPU:0 before, /device:TPU:25 now
where the time goes in v1:
time: 96.2 us; the launch traced here: 95.9 us
  Pallas kernels  77.7 us (81%)
  local copies, waits for them, and re-layouts  9.54 us (10%)
  between operations  8.42 us (9%)
    pallas_call x1, Pallas kernels, one_wave(): remote(functools.partial(reduce_kernel, sizes), 2, 3, [shape(count, round...  43.1 us
    pallas_call x1, Pallas kernels, one_wave(): remote(functools.partial(ratio_kernel, sizes), 1, 3, [shape(modes, quarte...  17.5 us
    pallas_call x1, Pallas kernels, one_wave(): remote(functools.partial(fetch_kernel, sizes), 0, 2, [shape(tiles, rounds...  11.6 us
    unnamed x27, local copies, waits for them, and re-layouts  7.02 us

profile of v1, /device:TPU:25, one launch (start us, length us, event | category | flops | bytes accessed | tf_op | source)
XLA Modules:
  0.0 95.9 jit_solution(1510198554804891738)
XLA Ops:
  0.6 0.7 copy-done.11
  1.3 0.1 and_select_fusion
  1.4 0.7 fusion.4
  9.7 1.5 %constant_dynamic-slice_fusion.3 = (f32[4,1,16,2,384]{4,3,2,1,0:T(2,128)S(1)}, f32[4,1,16,2,384]{4,3,2,1,0:T(2,128)S(1)}, f32[4,1,16,2,384]{4,3,2,1,0:T(2,128)S(1)}, f32[4,1,16,2,384]{4,3,2,1,0:T(2,128)S(1)}) fusion(f32[8,1,16,2,384]{4,3,2,1,0:T(2,128)} %param.8, s32[]{:T(128)S(6)} %select_n.48, s32[]{:T(128)S(6)} %select_n.50, s32[]{:T(128)S(6)} %select_n.49, ...), kind=kLoop, calls=%fused_computation.20 | loop fusion | bytes 1572880 | tf_op jit(solution)/shard_map/dynamic-slice.5 | solution.py:621
  11.3 0.0 copy-start.3
  11.3 0.0 copy-start.4
  11.3 0.1 pad_maximum_fusion.rows_ref
  11.4 0.9 copy-done
  12.3 11.6 %shard_map.95 = (f32[4,4,2,16,384]{4,3,2,1,0:T(8,128)S(1)}, f32[4,32,256]{2,1,0:T(8,128)S(1)}) custom-call(f32[4,4,2,16,384]{4,3,2,1,0:T(8,128)S(1)} %pad_maximum_fusion.rows_ref, f32[32,256]{1,0:T(8,128)S(1)} %fusion.square_ref), custom_call_target="tpu_custom_call" | custom-call | tf_op jit(solution)/shard_map/pallas_call | solution.py:532
  23.9 0.9 copy-done.5
  24.8 0.2 fusion.1.place_ref
  25.1 1.1 %copy-done.6 = f32[4,4,2,16,384]{4,3,2,1,0:T(8,128)S(1)} copy-done((f32[4,4,2,16,384]{4,3,2,1,0:T(8,128)S(1)}, f32[4,4,2,16,384]{4,3,2,1,0:T(8,128)}, u32[]{:S(2)}) %copy-start.6) | copy-done | bytes 786456
  26.2 1.8 %shard_map.96 = (f32[256,512]{1,0:T(8,128)S(1)}, f32[256,512]{1,0:T(8,128)S(1)}, f32[256,256]{1,0:T(8,128)S(1)}, f32[32,256]{1,0:T(8,128)S(1)}) custom-call(s32[2]{0:T(128)S(1)} %fusion.1.place_ref, f32[4,4,2,16,384]{4,3,2,1,0:T(8,128)S(1)} %copy-done.6, f32[4,32,256]{2,1,0:T(8,128)S(1)} %get-tuple-element.15.squares_ref, f32[256,512]{1,0:T(8,128)S(1)} %bitcast.57, ...), custom_call_target="tpu_custom_call" | custom-call | tf_op jit(solution)/shard_map/pallas_call | solution.py:539
  28.1 17.5 %shard_map.97 = (f32[4,64,256]{2,1,0:T(8,128)S(1)}, f32[8,32,256]{2,1,0:T(8,128)S(1)}) custom-call(f32[4,64,256]{2,1,0:T(8,128)S(1)} %bitcast.66, f32[32,256]{1,0:T(8,128)S(1)} %get-tuple-element.17.square_ref, f32[4,64,256]{2,1,0:T(8,128)S(1)} %bitcast.65), custom_call_target="tpu_custom_call" | custom-call | tf_op jit(solution)/shard_map/pallas_call | solution.py:549
  45.6 0.0 copy-start.8
  45.6 0.7 copy-done.8
  46.3 1.8 %shard_map.98 = (f32[4,4,16,512]{3,2,1,0:T(8,128)S(1)}, f32[256,768]{1,0:T(8,128)S(1)}) custom-call(s32[2]{0:T(128)S(1)} %fusion.1.place_ref, f32[256,256]{1,0:T(8,128)S(1)} %bitcast.64, f32[256,512]{1,0:T(8,128)S(1)} %get-tuple-element.19.far_ref, f32[256,512]{1,0:T(8,128)S(1)} %get-tuple-element.20.window_ref, f32[256,512]{1,0:T(8,128)S(1)} %bitcast.58, ...), custom_call_target="tpu_custom_call" | custom-call | tf_op jit(solution)/shard_map/pallas_call | solution.py:562
  48.1 43.1 %shard_map.99 = (f32[8,4,16,512]{3,2,1,0:T(8,128)S(1)}, f32[8,32,512]{2,1,0:T(8,128)S(1)}) custom-call(f32[4,4,16,512]{3,2,1,0:T(8,128)S(1)} %get-tuple-element.21.terms_ref, f32[8,32,768]{2,1,0:T(8,128)S(1)} %bitcast.62, f32[8,32,512]{2,1,0:T(8,128)S(1)} %bitcast.59), custom_call_target="tpu_custom_call" | custom-call | tf_op jit(solution)/shard_map/pallas_call | solution.py:567
  91.2 0.1 copy.42
  91.3 0.1 add_bitcast_fusion
  91.4 0.9 copy-done.9
  92.3 1.8 %shard_map.100 = f32[8,2,16,384]{3,2,1,0:T(8,128)S(1)} custom-call(s32[9,2]{1,0:T(8,128)S(1)} %pad_add_fusion.places_ref, f32[8,4,16,512]{3,2,1,0:T(8,128)S(1)} %get-tuple-element.23.all_ref, f32[16,16,256]{2,1,0:T(8,128)S(1)} %bitcast.67, f32[8,2,16,384]{3,2,1,0:T(8,128)S(1)} %bitcast.61), custom_call_target="tpu_custom_call" | custom-call | tf_op jit(solution)/shard_map/pallas_call | solution.py:587
  94.1 0.9 copy.48
  95.1 0.8 copy.56
  (24 shorter events, 0.2 us)
Async XLA Ops:
  0.6 0.7 copy-start.11
  11.2 1.0 %copy-start = (f32[1,256,512]{2,1,0:T(8,128)S(1)}, f32[1,256,512]{2,1,0:T(8,128)}, u32[]{:S(2)}) copy-start(f32[1,256,512]{2,1,0:T(8,128)} %param.9) | copy-start | bytes 1572868
  11.3 13.8 %copy-start.3 = (bf16[512,512]{1,0:T(8,128)(2,1)S(1)}, bf16[512,512]{1,0:T(8,128)(2,1)}, u32[]{:S(2)}) copy-start(bf16[512,512]{1,0:T(8,128)(2,1)} %constant.77.clone.gh) | copy-start | bytes 1572868
  11.3 13.8 %copy-start.4 = (bf16[512,512]{1,0:T(8,128)(2,1)S(1)}, bf16[512,512]{1,0:T(8,128)(2,1)}, u32[]{:S(2)}) copy-start(bf16[512,512]{1,0:T(8,128)(2,1)} %constant.78.clone.gl) | copy-start | bytes 1572868
  12.3 12.7 %copy-start.1 = (bf16[512,512]{1,0:T(8,128)(2,1)S(1)}, bf16[512,512]{1,0:T(8,128)(2,1)}, u32[]{:S(2)}) copy-start(bf16[512,512]{1,0:T(8,128)(2,1)} %constant.75.clone.rh) | copy-start | bytes 1572868
  12.3 12.8 %copy-start.2 = (bf16[512,512]{1,0:T(8,128)(2,1)S(1)}, bf16[512,512]{1,0:T(8,128)(2,1)}, u32[]{:S(2)}) copy-start(bf16[512,512]{1,0:T(8,128)(2,1)} %constant.76.clone.rl) | copy-start | bytes 1572868
  23.9 0.9 copy-start.5
  25.1 1.1 %copy-start.6 = (f32[4,4,2,16,384]{4,3,2,1,0:T(8,128)S(1)}, f32[4,4,2,16,384]{4,3,2,1,0:T(8,128)}, u32[]{:S(2)}) copy-start(f32[4,4,2,16,384]{4,3,2,1,0:T(8,128)} %copy-done.5) | copy-start | bytes 2359300
  26.2 1.8 %copy-start.7 = (f32[1,256,256]{2,1,0:T(8,128)S(1)}, f32[1,256,256]{2,1,0:T(8,128)}, u32[]{:S(2)}) copy-start(f32[1,256,256]{2,1,0:T(8,128)} %param.10) | copy-start | bytes 786436
  45.6 0.7 copy-start.8
  48.1 43.3 %copy-start.10 = (f32[8,1,16,2,384]{4,3,2,1,0:T(2,128)S(1)}, f32[8,1,16,2,384]{4,3,2,1,0:T(2,128)}, u32[]{:S(2)}) copy-start(f32[8,1,16,2,384]{4,3,2,1,0:T(2,128)} %param.8) | copy-start | bytes 1179652
  91.4 1.0 copy-start.9

commit v2 on v1

--- a/solution.py
+++ b/solution.py
@@ -275,34 +275,47 @@
     return {"scan": peer // tiles, "tile": lax.rem(peer, tiles)}
 
 
-def any_id(tiles, modes, peer):
-    return {
-        "scan": peer // (tiles * modes),
-        "tile": lax.rem(peer // modes, tiles),
-        "mode": lax.rem(peer, modes),
-    }
-
-
-def fetch_kernel(sizes, rows_ref, square_ref, got_ref, squares_ref, send, recv, send_p, recv_p):
+def round_id(scans, peer):
+    return {"scan": lax.rem(peer, scans), "mode": peer // scans}
+
+
+def place_of(places_ref, index, block):
+    return places_ref[0, index] // block, places_ref[1, index]
+
+
+def fetch_kernel(
+    sizes, places_ref, object_ref, probe_ref, got_ref, squares_ref,
+    rows, square, send, recv, send_p, recv_p,
+):
     scans, tiles, modes = sizes
-    tile, mode = lax.axis_index("tile"), lax.axis_index("mode")
+    scan, tile, mode = lax.axis_index("scan"), lax.axis_index("tile"), lax.axis_index("mode")
+    block = object_ref.shape[2]
+    rounds = rows.shape[1]
+    for index in range(tiles):
+        start, _ = place_of(places_ref, scan * tiles + index, block)
+        first = (start + lax.rem(tile - start + tiles * block * block, tiles)) // tiles
+        rows[index] = object_ref[pl.ds(first, rounds)]
+    share = square.shape[0]
+    square[...] = power(probe_ref[pl.ds((scan * tiles + tile) * share, share)])
     greet([(tile, tiles, tile_id), (mode, modes, mode_id)])
-    copies = sends(tile, tiles, tile_id, lambda peer: rows_ref.at[peer], got_ref, send, recv)
-    copies += sends(mode, modes, mode_id, lambda peer: square_ref, squares_ref, send_p, recv_p)
-    got_ref[tile] = rows_ref[tile]
-    squares_ref[mode] = square_ref[...]
+    copies = sends(tile, tiles, tile_id, lambda peer: rows.at[peer], got_ref, send, recv)
+    copies += sends(mode, modes, mode_id, lambda peer: square, squares_ref, send_p, recv_p)
+    got_ref[tile] = rows[tile]
+    squares_ref[mode] = square[...]
     for copy in copies:
         copy.wait()
 
 
 def forward_kernel(
-    tiles, place_ref, got_ref, squares_ref, probe_ref, rh, rl, gh, gl,
+    sizes, places_ref, got_ref, squares_ref, probe_ref, rh, rl, gh, gl,
     window_ref, far_ref, power_ref, square_ref,
 ):
     width = probe_ref.shape[0]
     block = got_ref.shape[3]
     columns = got_ref.shape[4]
-    start, col = place_ref[0], place_ref[1]
+    tiles = sizes[1]
+    me = lax.axis_index("scan") * tiles + lax.axis_index("tile")
+    start, col = place_of(places_ref, me, block)
     shift = lax.rem(columns - col, columns)
     for index in range(width // block):
         owner = lax.rem(start + index, tiles)
@@ -345,12 +358,15 @@
 
 
 def inverse_kernel(
-    tiles, place_ref, ratio_ref, far_ref, window_ref, probe_ref, rh, rl, gh, gl,
+    sizes, places_ref, ratio_ref, far_ref, window_ref, probe_ref, rh, rl, gh, gl,
     terms_ref, mixed_ref,
 ):
     width = probe_ref.shape[0]
     block = terms_ref.shape[2]
-    start = place_ref[0]
+    tiles = sizes[1]
+    count = sizes[0] * tiles
+    me = lax.axis_index("scan") * tiles + lax.axis_index("tile")
+    start, _ = place_of(places_ref, me, block)
     ratio = ratio_ref[...]
     scaled = far_ref[...] * jnp.concatenate([ratio, ratio], 1)
     waves = left_product(rh[...], rl[...], right_product(scaled, gh[...], gl[...]))
@@ -358,118 +374,80 @@
     difference = waves - times(probe, window)
     terms = conj_times(probe, difference)
     for index in range(width // block):
-        owner = lax.rem(start + index, tiles)
-        terms_ref[owner, index // tiles] = terms[index * block : (index + 1) * block]
+        owner = lax.rem(start + index, count)
+        terms_ref[owner, index // count] = terms[index * block : (index + 1) * block]
     mixed_ref[...] = jnp.concatenate([conj_times(window, difference), power(window)], 1)
 
 
 def reduce_kernel(
-    sizes, terms_ref, mixed_ref, probe_ref, all_ref, next_ref,
-    got, got_p, summed,
-    send, recv, send_m, recv_m, send_b, recv_b, send_n, recv_n,
+    sizes, places_ref, terms_ref, mixed_ref, probe_ref, square_ref, object_ref,
+    out_ref, next_ref,
+    got_t, got_p, canvas, got_c,
+    send_t, recv_t, send_m, recv_m, send_c, recv_c, send_o, recv_o, send_n, recv_n,
 ):
     scans, tiles, modes = sizes
-    width2 = probe_ref.shape[-1]
     count = scans * tiles
+    rounds, block, width2 = terms_ref.shape[1:]
+    width = width2 // 2
+    columns = object_ref.shape[-1]
     scan, tile, mode = lax.axis_index("scan"), lax.axis_index("tile"), lax.axis_index("mode")
     me = scan * tiles + tile
+    cycle = scan + scans * mode
     id_of = functools.partial(pattern_id, tiles)
-    greet([(me * modes + mode, count * modes, functools.partial(any_id, tiles, modes))])
-    first = sends(mode, modes, mode_id, lambda peer: terms_ref.at[peer], got, send, recv)
-    second = sends(me, count, id_of, lambda peer: mixed_ref.at[peer], got_p, send_m, recv_m)
-    got[mode] = terms_ref[mode]
+    id_round = functools.partial(round_id, scans)
+    greet([(me, count, id_of), (cycle, scans * modes, id_round)])
+    moves_t = sends(me, count, id_of, lambda peer: terms_ref.at[peer], got_t, send_t, recv_t)
+    moves_p = sends(me, count, id_of, lambda peer: mixed_ref.at[peer], got_p, send_m, recv_m)
+    got_t[me] = terms_ref[me]
     got_p[me] = mixed_ref[me]
-    for copy in first:
-        copy.wait()
-    total = got[0]
-    for index in range(1, modes):
-        total = total + got[index]
-    summed[...] = total
-    mine = tile == mode
-    copies = []
-    for scan_step in range(scans):
-        for mode_step in range(modes):
-            slot = scan_step * modes + mode_step
-            copy = pltpu.make_async_remote_copy(
-                src_ref=summed,
-                dst_ref=all_ref.at[me],
-                send_sem=send_b.at[slot],
-                recv_sem=recv_b.at[me],
-                device_id={
-                    "scan": lax.rem(scan + scan_step, scans),
-                    "tile": mode,
-                    "mode": lax.rem(mode + mode_step, modes),
-                },
-                device_id_type=MESH,
-            )
-            copies.append(copy)
-            if slot == 0:
-                pl.when(jnp.logical_not(mine))(copy.start)
-            else:
-                copy.start()
-
-    @pl.when(mine)
-    def _():
-        all_ref[me] = summed[...]
-
-    for copy in second:
+    blank = jnp.zeros((block, columns - width), f32)
+    zero = jnp.zeros((block, columns), f32)
+
+    def spread(piece, col):
+        return pltpu.roll(jnp.concatenate([piece, blank], 1), col, 1)
+
+    weight = zero
+    for index in range(count):
+        start, col = place_of(places_ref, index, block)
+        which = me + count * mode - start
+        inside = jnp.logical_and(which >= 0, which < count * rounds)
+        piece = square_ref[jnp.clip(which, 0, count * rounds - 1)]
+        weight = weight + jnp.where(inside, spread(piece, col), 0.0)
+    for copy in moves_t:
+        copy.wait()
+    for part in range(2):
+        sums = [zero] * modes
+        for index in range(count):
+            start, col = place_of(places_ref, index, block)
+            first = (start + lax.rem(me - start + count * block * block, count)) // count
+            for step in range(rounds):
+                piece = spread(got_t[index, step, :, part * width : (part + 1) * width], col)
+                for slot in range(modes):
+                    sums[slot] = sums[slot] + jnp.where(first + step == slot, piece, 0.0)
+        for slot in range(modes):
+            canvas[slot, part] = sums[slot]
+    moves_c = sends(mode, modes, mode_id, lambda peer: canvas.at[peer], got_c, send_c, recv_c)
+    got_c[mode] = canvas[mode]
+    for copy in moves_c:
+        copy.wait()
+    for part in range(2):
+        total = got_c[0, part]
+        for index in range(1, modes):
+            total = total + got_c[index, part]
+        out_ref[cycle, part] = object_ref[cycle, part] + total / (weight + damping)
+    last = sends(
+        cycle, scans * modes, id_round, lambda peer: out_ref.at[cycle], out_ref, send_o, recv_o
+    )
+    for copy in moves_p:
         copy.wait()
     totals = got_p[0]
     for index in range(1, count):
         totals = totals + got_p[index]
     divisor = totals[:, width2:]
     next_ref[me] = probe_ref[me] + totals[:, :width2] / jnp.concatenate([divisor, divisor], 1)
-    last = sends(me, count, id_of, lambda peer: next_ref.at[me], next_ref, send_n, recv_n)
-    for slot, copy in enumerate(copies):
-        if slot == 0:
-            pl.when(jnp.logical_not(mine))(copy.wait_send)
-        else:
-            copy.wait_send()
-    for source in range(count):
-
-        def arrived(source=source):
-            pltpu.make_async_remote_copy(
-                src_ref=summed,
-                dst_ref=all_ref.at[source],
-                send_sem=send_b.at[0],
-                recv_sem=recv_b.at[source],
-                device_id={"mode": mode},
-                device_id_type=MESH,
-            ).wait_recv()
-
-        pl.when(jnp.logical_not(jnp.logical_and(mine, me == source)))(arrived)
+    last += sends(me, count, id_of, lambda peer: next_ref.at[me], next_ref, send_n, recv_n)
     for copy in last:
         copy.wait()
-
-
-def update_kernel(tiles, places_ref, all_ref, square_ref, object_ref, out_ref, weight):
-    count, rounds, block, width2 = all_ref.shape
-    width = width2 // 2
-    columns = object_ref.shape[-1]
-    tile = places_ref[count, 0]
-    out_ref[...] = jnp.zeros_like(out_ref)
-    weight[...] = jnp.zeros_like(weight)
-    blank = jnp.zeros((block, columns - width), f32)
-
-    def add(pattern, carry):
-        start, col = places_ref[pattern, 0], places_ref[pattern, 1]
-        offset = lax.rem(tile - start + tiles * block * block, tiles)
-        cycle = (start + offset) // tiles
-        for index in range(rounds):
-            for part in range(2):
-                piece = all_ref[pattern, index, :, part * width : (part + 1) * width]
-                out_ref[cycle + index, part] += pltpu.roll(
-                    jnp.concatenate([piece, blank], 1), col, 1
-                )
-            weight[cycle + index] += pltpu.roll(
-                jnp.concatenate([square_ref[offset + tiles * index], blank], 1), col, 1
-            )
-        return carry
-
-    lax.fori_loop(0, count, add, 0)
-    divisor = weight[...] + damping
-    for part in range(2):
-        out_ref[:, part] = object_ref[:, part] + out_ref[:, part] / divisor
 
 
 def shape(*dims):
@@ -495,7 +473,7 @@
     return pl.pallas_call(
         kernel,
         out_shape=outs,
-        in_specs=[VMEM] * inputs,
+        in_specs=inputs,
         out_specs=[VMEM] * len(outs),
         scratch_shapes=scratch,
         compiler_params=pltpu.CompilerParams(
@@ -513,31 +491,23 @@
     rounds = blocks // tiles
     share = width // count
     quarter = width // modes
-    scan, tile = lax.axis_index("scan"), lax.axis_index("tile")
-    me = scan * tiles + tile
-    starts = positions[:, 0] // block
-    places = jnp.stack([starts, positions[:, 1]], 1)
-    place_now = lax.dynamic_index_in_dim(places, me, 0, keepdims=False)
+    places = positions.T
     probe = probe_modes[0]
     planar = jnp.swapaxes(object_field[:, 0], 1, 2)
-    group = lax.dynamic_slice_in_dim(starts, scan * tiles, tiles, 0)
-    first_cycle = (group + jnp.mod(tile - group, tiles)) // tiles
-    rows = jnp.stack(
-        [
-            lax.dynamic_slice_in_dim(planar, first_cycle[index], rounds, 0)
-            for index in range(tiles)
-        ]
-    )
-    square = power(lax.dynamic_slice_in_dim(probe, me * share, share, 0))
     got, squares = remote(
         functools.partial(fetch_kernel, sizes),
         0,
-        2,
+        [SMEM, VMEM, VMEM],
         [shape(tiles, rounds, 2, block, columns), shape(modes, share, width)],
-        [dma(tiles - 1), dma(tiles - 1), dma(modes - 1), dma(modes - 1)],
-    )(rows, square)
+        [
+            pltpu.VMEM((tiles, rounds, 2, block, columns), f32),
+            pltpu.VMEM((share, width), f32),
+        ]
+        + [dma(tiles - 1)] * 2
+        + [dma(modes - 1)] * 2,
+    )(places, planar, probe)
     window, far, strength, square = local(
-        functools.partial(forward_kernel, tiles),
+        functools.partial(forward_kernel, sizes),
         [SMEM] + [VMEM] * 7,
         [
             shape(width, 2 * width),
@@ -545,11 +515,11 @@
             shape(width, width),
             shape(share, width),
         ],
-    )(place_now, got, squares, probe, *tables)
+    )(places, got, squares, probe, *tables)
     ratio, squares = remote(
         functools.partial(ratio_kernel, sizes),
         1,
-        3,
+        [VMEM] * 3,
         [shape(modes, quarter, width), shape(count, share, width)],
         [pltpu.VMEM((modes, quarter, width), f32)]
         + [dma(modes - 1)] * 4
@@ -559,39 +529,32 @@
         square,
         intensities.reshape(modes, quarter, width),
     )
+    parts = blocks // count
     terms, mixed = local(
-        functools.partial(inverse_kernel, tiles),
+        functools.partial(inverse_kernel, sizes),
         [SMEM] + [VMEM] * 8,
-        [shape(tiles, rounds, block, 2 * width), shape(width, 3 * width)],
-    )(place_now, ratio.reshape(width, width), far, window, probe, *tables)
-    everything, probe_next = remote(
+        [shape(count, parts, block, 2 * width), shape(width, 3 * width)],
+    )(places, ratio.reshape(width, width), far, window, probe, *tables)
+    updated, probe_next = remote(
         functools.partial(reduce_kernel, sizes),
         2,
-        3,
-        [shape(count, rounds, block, 2 * width), shape(count, share, 2 * width)],
+        [SMEM] + [VMEM] * 5,
+        [shape(cycles, 2, block, columns), shape(count, share, 2 * width)],
         [
-            pltpu.VMEM((modes, rounds, block, 2 * width), f32),
+            pltpu.VMEM((count, parts, block, 2 * width), f32),
             pltpu.VMEM((count, share, 3 * width), f32),
-            pltpu.VMEM((rounds, block, 2 * width), f32),
+            pltpu.VMEM((modes, 2, block, columns), f32),
+            pltpu.VMEM((modes, 2, block, columns), f32),
         ]
+        + [dma(count - 1)] * 4
         + [dma(modes - 1)] * 2
-        + [dma(count - 1)] * 2
-        + [dma(scans * modes), dma(count)]
+        + [dma(cycles - 1)] * 2
         + [dma(count - 1)] * 2,
     )(
+        places,
         terms,
         mixed.reshape(count, share, 3 * width),
         probe.reshape(count, share, 2 * width),
-    )
-    own = jnp.stack([tile, tile])[None].astype(jnp.int32)
-    updated = local(
-        functools.partial(update_kernel, tiles),
-        [SMEM] + [VMEM] * 3,
-        shape(cycles, 2, block, columns),
-        [pltpu.VMEM((cycles, block, columns), f32)],
-    )(
-        jnp.concatenate([places, own], 0),
-        everything,
         squares.reshape(blocks, block, width),
         planar,
     )
@@ -612,9 +575,10 @@
     def run(object_field, probe_modes, intensities, positions):
         body = on_device
         if (
-            sizes[1] == sizes[2]
+            object_field.shape[0] == sizes[0] * sizes[2]
             and probe_modes.shape[0] == sizes[2]
             and intensities.shape[0] == sizes[0] * sizes[1]
+            and probe_modes.shape[1] % (object_field.shape[2] * sizes[0] * sizes[1]) == 0
         ):
             tables = [jnp.asarray(table) for table in split_tables(probe_modes.shape[1])]
             body = functools.partial(one_wave, sizes, tables)

time: 96.2 us -> 70.8 us (0.74)
  the two profiles are of different devices: /device:TPU:25 before, /device:TPU:0 now
where the time goes in v2:
time: 70.8 us; the launch traced here: 70.3 us
  Pallas kernels  63.9 us (90%)
  local copies, waits for them, and re-layouts  5.7 us (8%)
  between operations  0.76 us (1%)
    pallas_call x1, Pallas kernels, one_wave(): remote(functools.partial(reduce_kernel, sizes), 2, [SMEM] + [VMEM] * 5, [...  28.9 us
    pallas_call x1, Pallas kernels, one_wave(): remote(functools.partial(ratio_kernel, sizes), 1, [VMEM] * 3, [shape(mode...  17 us
    pallas_call x1, Pallas kernels, one_wave(): remote(functools.partial(fetch_kernel, sizes), 0, [SMEM, VMEM, VMEM], [sh...  14.2 us
    unnamed x21, local copies, waits for them, and re-layouts  5.7 us
    pallas_call x1, Pallas kernels, one_wave(): local(functools.partial(forward_kernel, sizes), [SMEM] + [VMEM] * 7, [sha...  1.88 us
    pallas_call x1, Pallas kernels, one_wave(): local(functools.partial(inverse_kernel, sizes), [SMEM] + [VMEM] * 8, [sha...  1.87 us

profile of v2, /device:TPU:0, one launch (start us, length us, event | category | flops | bytes accessed | tf_op | source)
XLA Modules:
  0.0 70.3 jit_solution(16067033557732773035)
XLA Ops:
  0.6 0.0 copy-start
  0.6 0.0 copy-start.2
  0.7 1.1 %copy.13 = f32[8,1,16,2,384]{4,2,3,0,1:T(8,128)S(1)} copy(f32[8,1,16,2,384]{4,3,2,1,0:T(2,128)} %param.8) | data formatting | bytes 786432 | tf_op args[0]
  1.8 0.0 copy-start.1
  1.8 0.0 copy-done
  1.8 0.0 copy-start.8
  1.8 0.7 %copy-done.8 = s32[8,2]{0,1:T(2,128)S(1)} copy-done((s32[8,2]{0,1:T(2,128)S(1)}, s32[8,2]{0,1:T(2,128)}, u32[]{:S(2)}) %copy-start.8) | copy-done | bytes 88
  2.5 14.2 %shard_map.95 = (f32[4,4,2,16,384]{4,3,2,1,0:T(8,128)S(1)}, f32[4,32,256]{2,1,0:T(8,128)S(1)}) custom-call(s32[2,8]{1,0:T(2,128)S(1)} %bitcast.30, f32[8,2,16,384]{3,2,1,0:T(8,128)S(1)} %bitcast.21, f32[256,512]{1,0:T(8,128)S(1)} %bitcast.17), custom_call_target="tpu_custom_call" | custom-call | tf_op jit(solution)/shard_map/pallas_call | solution.py:497
  16.7 0.0 copy-done.2
  16.8 0.0 copy-done.1
  16.8 0.0 copy-start.3
  16.8 1.0 %copy-done.3 = bf16[512,512]{1,0:T(8,128)(2,1)S(1)} copy-done((bf16[512,512]{1,0:T(8,128)(2,1)S(1)}, bf16[512,512]{1,0:T(8,128)(2,1)}, u32[]{:S(2)}) %copy-start.3) | copy-done | bytes 524312
  17.8 0.0 copy-start.5
  17.8 1.0 %copy-done.5 = bf16[512,512]{1,0:T(8,128)(2,1)S(1)} copy-done((bf16[512,512]{1,0:T(8,128)(2,1)S(1)}, bf16[512,512]{1,0:T(8,128)(2,1)}, u32[]{:S(2)}) %copy-start.5) | copy-done | bytes 524312
  18.9 1.9 %shard_map.96 = (f32[256,512]{1,0:T(8,128)S(1)}, f32[256,512]{1,0:T(8,128)S(1)}, f32[256,256]{1,0:T(8,128)S(1)}, f32[32,256]{1,0:T(8,128)S(1)}) custom-call(s32[2,8]{1,0:T(2,128)S(1)} %bitcast.31, f32[4,4,2,16,384]{4,3,2,1,0:T(8,128)S(1)} %get-tuple-element.14.got_ref, f32[4,32,256]{2,1,0:T(8,128)S(1)} %get-tuple-element.15.squares_ref, ...), custom_call_target="tpu_custom_call" | custom-call | tf_op jit(solution)/shard_map/pallas_call | solution.py:509
  20.7 0.0 copy-start.4
  20.8 0.0 copy-done.7
  20.8 17.0 %shard_map.97 = (f32[4,64,256]{2,1,0:T(8,128)S(1)}, f32[8,32,256]{2,1,0:T(8,128)S(1)}) custom-call(f32[4,64,256]{2,1,0:T(8,128)S(1)} %bitcast.29, f32[32,256]{1,0:T(8,128)S(1)} %get-tuple-element.17.square_ref, f32[4,64,256]{2,1,0:T(8,128)S(1)} %bitcast.28), custom_call_target="tpu_custom_call" | custom-call | tf_op jit(solution)/shard_map/pallas_call | solution.py:519
  37.8 0.0 copy-done.6
  37.8 0.0 copy-done.4
  37.8 1.9 %shard_map.98 = (f32[8,2,16,512]{3,2,1,0:T(8,128)S(1)}, f32[256,768]{1,0:T(8,128)S(1)}) custom-call(s32[2,8]{1,0:T(2,128)S(1)} %bitcast.32, f32[256,256]{1,0:T(8,128)S(1)} %bitcast.27, f32[256,512]{1,0:T(8,128)S(1)} %get-tuple-element.19.far_ref, f32[256,512]{1,0:T(8,128)S(1)} %get-tuple-element.20.window_ref, f32[256,512]{1,0:T(8,128)S(1)} %bitcast.19, ...), custom_call_target="tpu_custom_call" | custom-call | tf_op jit(solution)/shard_map/pallas_call | solution.py:533
  39.7 28.9 %shard_map.99 = (f32[8,2,16,384]{3,2,1,0:T(8,128)S(1)}, f32[8,32,512]{2,1,0:T(8,128)S(1)}) custom-call(s32[2,8]{1,0:T(2,128)S(1)} %bitcast.33, f32[8,2,16,512]{3,2,1,0:T(8,128)S(1)} %get-tuple-element.21.terms_ref, f32[8,32,768]{2,1,0:T(8,128)S(1)} %bitcast.23, f32[8,32,512]{2,1,0:T(8,128)S(1)} %bitcast.20, f32[16,16,256]{2,1,0:T(8,128)S(1)} %bitcast.26, ...), custom_call_target="tpu_custom_call" | custom-call | tf_op jit(solution)/shard_map/pallas_call | solution.py:538
  68.6 0.9 %copy.11 = f32[8,1,16,2,384]{4,3,2,1,0:T(2,128)} copy(f32[8,1,16,2,384]{4,2,3,0,1:T(8,128)S(1)} %bitcast.25) | data formatting | bytes 786432
  69.5 0.8 %copy.15 = f32[1,256,512]{2,1,0:T(8,128)} copy(f32[1,256,512]{2,1,0:T(8,128)S(1)} %bitcast.24) | data formatting | bytes 1048576
  (2 shorter events, 0.0 us)
Async XLA Ops:
  0.6 1.2 %copy-start = (f32[1,256,512]{2,1,0:T(8,128)S(1)}, f32[1,256,512]{2,1,0:T(8,128)}, u32[]{:S(2)}) copy-start(f32[1,256,512]{2,1,0:T(8,128)} %param.9) | copy-start | bytes 1572868
  0.6 16.1 %copy-start.2 = (bf16[512,512]{1,0:T(8,128)(2,1)S(1)}, bf16[512,512]{1,0:T(8,128)(2,1)}, u32[]{:S(2)}) copy-start(bf16[512,512]{1,0:T(8,128)(2,1)} %constant.10.clone.gh) | copy-start | bytes 1572868
  1.8 15.0 %copy-start.1 = (bf16[512,512]{1,0:T(8,128)(2,1)S(1)}, bf16[512,512]{1,0:T(8,128)(2,1)}, u32[]{:S(2)}) copy-start(bf16[512,512]{1,0:T(8,128)(2,1)} %constant.11.clone.gl) | copy-start | bytes 1572868
  1.8 0.7 %copy-start.8 = (s32[8,2]{0,1:T(2,128)S(1)}, s32[8,2]{0,1:T(2,128)}, u32[]{:S(2)}) copy-start(s32[8,2]{0,1:T(2,128)} %param.11) | copy-start | bytes 196
  16.8 1.0 %copy-start.3 = (bf16[512,512]{1,0:T(8,128)(2,1)S(1)}, bf16[512,512]{1,0:T(8,128)(2,1)}, u32[]{:S(2)}) copy-start(bf16[512,512]{1,0:T(8,128)(2,1)} %constant.9.clone.rl) | copy-start | bytes 1572868
  17.8 1.0 %copy-start.5 = (bf16[512,512]{1,0:T(8,128)(2,1)S(1)}, bf16[512,512]{1,0:T(8,128)(2,1)}, u32[]{:S(2)}) copy-start(bf16[512,512]{1,0:T(8,128)(2,1)} %constant.8.clone.rh) | copy-start | bytes 1572868
  18.9 1.9 %copy-start.7 = (f32[1,256,256]{2,1,0:T(8,128)S(1)}, f32[1,256,256]{2,1,0:T(8,128)}, u32[]{:S(2)}) copy-start(f32[1,256,256]{2,1,0:T(8,128)} %param.10) | copy-start | bytes 786436
  18.9 18.9 %copy-start.6 = (bf16[512,512]{1,0:T(8,128)(2,1)S(1)}, bf16[512,512]{1,0:T(8,128)(2,1)}, u32[]{:S(2)}) copy-start(bf16[512,512]{1,0:T(8,128)(2,1)} %constant.8.clone.rh) | copy-start | bytes 1572868
  20.7 17.0 %copy-start.4 = (bf16[512,512]{1,0:T(8,128)(2,1)S(1)}, bf16[512,512]{1,0:T(8,128)(2,1)}, u32[]{:S(2)}) copy-start(bf16[512,512]{1,0:T(8,128)(2,1)} %constant.9.clone.rl) | copy-start | bytes 1572868

commit v3 on v2

--- a/solution.py
+++ b/solution.py
@@ -290,11 +290,14 @@
     scans, tiles, modes = sizes
     scan, tile, mode = lax.axis_index("scan"), lax.axis_index("tile"), lax.axis_index("mode")
     block = object_ref.shape[2]
-    rounds = rows.shape[1]
+    columns = object_ref.shape[3]
+    rounds, width = rows.shape[1], rows.shape[4]
     for index in range(tiles):
-        start, _ = place_of(places_ref, scan * tiles + index, block)
+        start, col = place_of(places_ref, scan * tiles + index, block)
         first = (start + lax.rem(tile - start + tiles * block * block, tiles)) // tiles
-        rows[index] = object_ref[pl.ds(first, rounds)]
+        piece = object_ref[pl.ds(first, rounds)].reshape(rounds * 2 * block, columns)
+        piece = pltpu.roll(piece, lax.rem(columns - col, columns), 1)[:, :width]
+        rows[index] = piece.reshape(rounds, 2, block, width)
     share = square.shape[0]
     square[...] = power(probe_ref[pl.ds((scan * tiles + tile) * share, share)])
     greet([(tile, tiles, tile_id), (mode, modes, mode_id)])
@@ -308,32 +311,30 @@
 
 def forward_kernel(
     sizes, places_ref, got_ref, squares_ref, probe_ref, rh, rl, gh, gl,
-    window_ref, far_ref, power_ref, square_ref,
+    window_ref, far_ref, power_ref, square_ref, bright_ref,
 ):
     width = probe_ref.shape[0]
     block = got_ref.shape[3]
-    columns = got_ref.shape[4]
     tiles = sizes[1]
     me = lax.axis_index("scan") * tiles + lax.axis_index("tile")
-    start, col = place_of(places_ref, me, block)
-    shift = lax.rem(columns - col, columns)
+    start, _ = place_of(places_ref, me, block)
     for index in range(width // block):
         owner = lax.rem(start + index, tiles)
         for part in range(2):
-            piece = got_ref[owner, index // tiles, part]
             window_ref[index * block : (index + 1) * block, part * width : (part + 1) * width] = (
-                pltpu.roll(piece, shift, 1)[:, :width]
+                got_ref[owner, index // tiles, part]
             )
     waves = times(probe_ref[...], window_ref[...])
     far = left_product(gh[...], gl[...], right_product(waves, rh[...], rl[...]))
     far_ref[...] = far
     power_ref[...] = power(far)
     square_ref[...] = jnp.sum(squares_ref[...], axis=0)
+    bright_ref[...] = power(window_ref[...])
 
 
 def ratio_kernel(
-    sizes, power_ref, square_ref, measured_ref, ratio_ref, squares_ref,
-    got, send, recv, send_r, recv_r, send_p, recv_p,
+    sizes, power_ref, square_ref, bright_ref, measured_ref, ratio_ref, squares_ref, sum_ref,
+    got, got_b, send, recv, send_r, recv_r, send_p, recv_p, send_b, recv_b,
 ):
     scans, tiles, modes = sizes
     mode = lax.axis_index("mode")
@@ -342,6 +343,10 @@
     greet([(mode, modes, mode_id), (me, scans * tiles, id_of)])
     first = sends(mode, modes, mode_id, lambda peer: power_ref.at[peer], got, send, recv)
     other = sends(me, scans * tiles, id_of, lambda peer: square_ref, squares_ref, send_p, recv_p)
+    more = sends(
+        me, scans * tiles, id_of, lambda peer: bright_ref.at[peer], got_b, send_b, recv_b
+    )
+    got_b[me] = bright_ref[me]
     got[mode] = power_ref[mode]
     squares_ref[me] = square_ref[...]
     for copy in first:
@@ -353,7 +358,10 @@
     last = sends(
         mode, modes, mode_id, lambda peer: ratio_ref.at[mode], ratio_ref, send_r, recv_r
     )
-    for copy in last + other:
+    for copy in more + other:
+        copy.wait()
+    sum_ref[...] = jnp.sum(got_b[...], axis=0)
+    for copy in last:
         copy.wait()
 
 
@@ -376,11 +384,11 @@
     for index in range(width // block):
         owner = lax.rem(start + index, count)
         terms_ref[owner, index // count] = terms[index * block : (index + 1) * block]
-    mixed_ref[...] = jnp.concatenate([conj_times(window, difference), power(window)], 1)
+    mixed_ref[...] = conj_times(window, difference)
 
 
 def reduce_kernel(
-    sizes, places_ref, terms_ref, mixed_ref, probe_ref, square_ref, object_ref,
+    sizes, places_ref, terms_ref, mixed_ref, probe_ref, square_ref, bright_ref, object_ref,
     out_ref, next_ref,
     got_t, got_p, canvas, got_c,
     send_t, recv_t, send_m, recv_m, send_c, recv_c, send_o, recv_o, send_n, recv_n,
@@ -397,7 +405,6 @@
     id_round = functools.partial(round_id, scans)
     greet([(me, count, id_of), (cycle, scans * modes, id_round)])
     moves_t = sends(me, count, id_of, lambda peer: terms_ref.at[peer], got_t, send_t, recv_t)
-    moves_p = sends(me, count, id_of, lambda peer: mixed_ref.at[peer], got_p, send_m, recv_m)
     got_t[me] = terms_ref[me]
     got_p[me] = mixed_ref[me]
     blank = jnp.zeros((block, columns - width), f32)
@@ -415,6 +422,7 @@
         weight = weight + jnp.where(inside, spread(piece, col), 0.0)
     for copy in moves_t:
         copy.wait()
+    moves_p = sends(me, count, id_of, lambda peer: mixed_ref.at[peer], got_p, send_m, recv_m)
     for part in range(2):
         sums = [zero] * modes
         for index in range(count):
@@ -443,8 +451,8 @@
     totals = got_p[0]
     for index in range(1, count):
         totals = totals + got_p[index]
-    divisor = totals[:, width2:]
-    next_ref[me] = probe_ref[me] + totals[:, :width2] / jnp.concatenate([divisor, divisor], 1)
+    divisor = bright_ref[...]
+    next_ref[me] = probe_ref[me] + totals / jnp.concatenate([divisor, divisor], 1)
     last += sends(me, count, id_of, lambda peer: next_ref.at[me], next_ref, send_n, recv_n)
     for copy in last:
         copy.wait()
@@ -498,15 +506,15 @@
         functools.partial(fetch_kernel, sizes),
         0,
         [SMEM, VMEM, VMEM],
-        [shape(tiles, rounds, 2, block, columns), shape(modes, share, width)],
+        [shape(tiles, rounds, 2, block, width), shape(modes, share, width)],
         [
-            pltpu.VMEM((tiles, rounds, 2, block, columns), f32),
+            pltpu.VMEM((tiles, rounds, 2, block, width), f32),
             pltpu.VMEM((share, width), f32),
         ]
         + [dma(tiles - 1)] * 2
         + [dma(modes - 1)] * 2,
     )(places, planar, probe)
-    window, far, strength, square = local(
+    window, far, strength, square, bright = local(
         functools.partial(forward_kernel, sizes),
         [SMEM] + [VMEM] * 7,
         [
@@ -514,35 +522,37 @@
             shape(width, 2 * width),
             shape(width, width),
             shape(share, width),
+            shape(width, width),
         ],
     )(places, got, squares, probe, *tables)
-    ratio, squares = remote(
+    ratio, squares, bright = remote(
         functools.partial(ratio_kernel, sizes),
         1,
-        [VMEM] * 3,
-        [shape(modes, quarter, width), shape(count, share, width)],
-        [pltpu.VMEM((modes, quarter, width), f32)]
+        [VMEM] * 4,
+        [shape(modes, quarter, width), shape(count, share, width), shape(share, width)],
+        [pltpu.VMEM((modes, quarter, width), f32), pltpu.VMEM((count, share, width), f32)]
         + [dma(modes - 1)] * 4
-        + [dma(count - 1)] * 2,
+        + [dma(count - 1)] * 4,
     )(
         strength.reshape(modes, quarter, width),
         square,
+        bright.reshape(count, share, width),
         intensities.reshape(modes, quarter, width),
     )
     parts = blocks // count
     terms, mixed = local(
         functools.partial(inverse_kernel, sizes),
         [SMEM] + [VMEM] * 8,
-        [shape(count, parts, block, 2 * width), shape(width, 3 * width)],
+        [shape(count, parts, block, 2 * width), shape(width, 2 * width)],
     )(places, ratio.reshape(width, width), far, window, probe, *tables)
     updated, probe_next = remote(
         functools.partial(reduce_kernel, sizes),
         2,
-        [SMEM] + [VMEM] * 5,
+        [SMEM] + [VMEM] * 6,
         [shape(cycles, 2, block, columns), shape(count, share, 2 * width)],
         [
             pltpu.VMEM((count, parts, block, 2 * width), f32),
-            pltpu.VMEM((count, share, 3 * width), f32),
+            pltpu.VMEM((count, share, 2 * width), f32),
             pltpu.VMEM((modes, 2, block, columns), f32),
             pltpu.VMEM((modes, 2, block, columns), f32),
         ]
@@ -553,9 +563,10 @@
     )(
         places,
         terms,
-        mixed.reshape(count, share, 3 * width),
+        mixed.reshape(count, share, 2 * width),
         probe.reshape(count, share, 2 * width),
         squares.reshape(blocks, block, width),
+        bright,
         planar,
     )
     new_object = jnp.swapaxes(updated, 1, 2)[:, None]

time: 70.8 us -> 67.1 us (0.948)
  Pallas kernels: 63.9 us -> 60.1 us
    pallas_call x1, Pallas kernels: 14.2 us -> 11.9 us  [one_wave(): remote(functools.partial(fetch_kernel, sizes), 0, [SMEM, VMEM, VMEM], [sh...]
    pallas_call x2, Pallas kernels: 45.9 us -> 44.6 us  [the longest x1 27.8 us: one_wave(): remote(functools.partial(reduce_kernel, sizes), 2, [SMEM] + [VMEM] * 6, [...]
where the time goes in v3:
time: 67.1 us; the launch traced here: 66.6 us
  Pallas kernels  60.1 us (90%)
  local copies, waits for them, and re-layouts  5.7 us (8%)
  between operations  0.76 us (1%)
    pallas_call x1, Pallas kernels, one_wave(): remote(functools.partial(reduce_kernel, sizes), 2, [SMEM] + [VMEM] * 6, [...  27.8 us
    pallas_call x1, Pallas kernels, one_wave(): remote(functools.partial(ratio_kernel, sizes), 1, [VMEM] * 4, [shape(mode...  16.8 us
    pallas_call x1, Pallas kernels, one_wave(): remote(functools.partial(fetch_kernel, sizes), 0, [SMEM, VMEM, VMEM], [sh...  11.9 us
    unnamed x21, local copies, waits for them, and re-layouts  5.7 us
    pallas_call x1, Pallas kernels, one_wave(): local(functools.partial(inverse_kernel, sizes), [SMEM] + [VMEM] * 8, [sha...  1.87 us
    pallas_call x1, Pallas kernels, one_wave(): local(functools.partial(forward_kernel, sizes), [SMEM] + [VMEM] * 7, [sha...  1.73 us

profile of v3, /device:TPU:0, one launch (start us, length us, event | category | flops | bytes accessed | tf_op | source)
XLA Modules:
  0.0 66.6 jit_solution(14293916725327577038)
XLA Ops:
  0.6 0.0 copy-start
  0.6 0.0 copy-start.2
  0.7 1.1 %copy.13 = f32[8,1,16,2,384]{4,2,3,0,1:T(8,128)S(1)} copy(f32[8,1,16,2,384]{4,3,2,1,0:T(2,128)} %param.8) | data formatting | bytes 786432 | tf_op args[0]
  1.8 0.0 copy-start.1
  1.8 0.0 copy-done
  1.8 0.0 copy-start.8
  1.8 0.7 %copy-done.8 = s32[8,2]{0,1:T(2,128)S(1)} copy-done((s32[8,2]{0,1:T(2,128)S(1)}, s32[8,2]{0,1:T(2,128)}, u32[]{:S(2)}) %copy-start.8) | copy-done | bytes 88
  2.5 11.9 %shard_map.95 = (f32[4,4,2,16,256]{4,3,2,1,0:T(8,128)S(1)}, f32[4,32,256]{2,1,0:T(8,128)S(1)}) custom-call(s32[2,8]{1,0:T(2,128)S(1)} %bitcast.32, f32[8,2,16,384]{3,2,1,0:T(8,128)S(1)} %bitcast.22, f32[256,512]{1,0:T(8,128)S(1)} %bitcast.18), custom_call_target="tpu_custom_call" | custom-call | tf_op jit(solution)/shard_map/pallas_call | solution.py:505
  14.5 0.0 copy-done.2
  14.5 0.0 copy-done.1
  14.5 0.0 copy-start.3
  14.5 1.0 %copy-done.3 = bf16[512,512]{1,0:T(8,128)(2,1)S(1)} copy-done((bf16[512,512]{1,0:T(8,128)(2,1)S(1)}, bf16[512,512]{1,0:T(8,128)(2,1)}, u32[]{:S(2)}) %copy-start.3) | copy-done | bytes 524312
  15.5 0.0 copy-start.5
  15.5 1.0 %copy-done.5 = bf16[512,512]{1,0:T(8,128)(2,1)S(1)} copy-done((bf16[512,512]{1,0:T(8,128)(2,1)S(1)}, bf16[512,512]{1,0:T(8,128)(2,1)}, u32[]{:S(2)}) %copy-start.5) | copy-done | bytes 524312
  16.6 1.7 %shard_map.96 = (f32[256,512]{1,0:T(8,128)S(1)}, f32[256,512]{1,0:T(8,128)S(1)}, f32[256,256]{1,0:T(8,128)S(1)}, f32[32,256]{1,0:T(8,128)S(1)}, f32[256,256]{1,0:T(8,128)S(1)}) custom-call(s32[2,8]{1,0:T(2,128)S(1)} %bitcast.33, f32[4,4,2,16,256]{4,3,2,1,0:T(8,128)S(1)} %get-tuple-element.16.got_ref, f32[4,32,256]{2,1,0:T(8,128)S(1)} %get-tuple-element.17.squares_ref, ...), custom_call_target="tpu_custom_call" | custom-call | tf_op jit(solution)/shard_map/pallas_call | solution.py:517
  18.3 0.0 copy-start.4
  18.3 0.0 copy-done.7
  18.3 16.8 %shard_map.97 = (f32[4,64,256]{2,1,0:T(8,128)S(1)}, f32[8,32,256]{2,1,0:T(8,128)S(1)}, f32[32,256]{1,0:T(8,128)S(1)}) custom-call(f32[4,64,256]{2,1,0:T(8,128)S(1)} %bitcast.29, f32[32,256]{1,0:T(8,128)S(1)} %get-tuple-element.19.square_ref, f32[8,32,256]{2,1,0:T(8,128)S(1)} %bitcast.30, f32[4,64,256]{2,1,0:T(8,128)S(1)} %bitcast.27), custom_call_target="tpu_custom_call" | custom-call | tf_op jit(solution)/shard_map/pallas_call | solution.py:528
  35.1 0.0 copy-done.6
  35.1 0.0 copy-done.4
  35.1 1.9 %shard_map.98 = (f32[8,2,16,512]{3,2,1,0:T(8,128)S(1)}, f32[256,512]{1,0:T(8,128)S(1)}) custom-call(s32[2,8]{1,0:T(2,128)S(1)} %bitcast.34, f32[256,256]{1,0:T(8,128)S(1)} %bitcast.28, f32[256,512]{1,0:T(8,128)S(1)} %get-tuple-element.22.far_ref, f32[256,512]{1,0:T(8,128)S(1)} %get-tuple-element.23.window_ref, f32[256,512]{1,0:T(8,128)S(1)} %bitcast.20, ...), custom_call_target="tpu_custom_call" | custom-call | tf_op jit(solution)/shard_map/pallas_call | solution.py:543
  37.0 27.8 %shard_map.99 = (f32[8,2,16,384]{3,2,1,0:T(8,128)S(1)}, f32[8,32,512]{2,1,0:T(8,128)S(1)}) custom-call(s32[2,8]{1,0:T(2,128)S(1)} %bitcast.35, f32[8,2,16,512]{3,2,1,0:T(8,128)S(1)} %get-tuple-element.24.terms_ref, f32[8,32,512]{2,1,0:T(8,128)S(1)} %bitcast.25, f32[8,32,512]{2,1,0:T(8,128)S(1)} %bitcast.21, f32[16,16,256]{2,1,0:T(8,128)S(1)} %bitcast.31, ...), custom_call_target="tpu_custom_call" | custom-call | tf_op jit(solution)/shard_map/pallas_call | solution.py:548
  64.8 0.9 %copy.11 = f32[8,1,16,2,384]{4,3,2,1,0:T(2,128)} copy(f32[8,1,16,2,384]{4,2,3,0,1:T(8,128)S(1)} %bitcast.26) | data formatting | bytes 786432
  65.8 0.8 %copy.15 = f32[1,256,512]{2,1,0:T(8,128)} copy(f32[1,256,512]{2,1,0:T(8,128)S(1)} %bitcast.24) | data formatting | bytes 1048576
  (2 shorter events, 0.0 us)
Async XLA Ops:
  0.6 1.2 %copy-start = (f32[1,256,512]{2,1,0:T(8,128)S(1)}, f32[1,256,512]{2,1,0:T(8,128)}, u32[]{:S(2)}) copy-start(f32[1,256,512]{2,1,0:T(8,128)} %param.9) | copy-start | bytes 1572868
  0.6 13.8 %copy-start.2 = (bf16[512,512]{1,0:T(8,128)(2,1)S(1)}, bf16[512,512]{1,0:T(8,128)(2,1)}, u32[]{:S(2)}) copy-start(bf16[512,512]{1,0:T(8,128)(2,1)} %constant.10.clone.gh) | copy-start | bytes 1572868
  1.8 12.7 %copy-start.1 = (bf16[512,512]{1,0:T(8,128)(2,1)S(1)}, bf16[512,512]{1,0:T(8,128)(2,1)}, u32[]{:S(2)}) copy-start(bf16[512,512]{1,0:T(8,128)(2,1)} %constant.11.clone.gl) | copy-start | bytes 1572868
  1.8 0.7 %copy-start.8 = (s32[8,2]{0,1:T(2,128)S(1)}, s32[8,2]{0,1:T(2,128)}, u32[]{:S(2)}) copy-start(s32[8,2]{0,1:T(2,128)} %param.11) | copy-start | bytes 196
  14.5 1.0 %copy-start.3 = (bf16[512,512]{1,0:T(8,128)(2,1)S(1)}, bf16[512,512]{1,0:T(8,128)(2,1)}, u32[]{:S(2)}) copy-start(bf16[512,512]{1,0:T(8,128)(2,1)} %constant.9.clone.rl) | copy-start | bytes 1572868
  15.5 1.0 %copy-start.5 = (bf16[512,512]{1,0:T(8,128)(2,1)S(1)}, bf16[512,512]{1,0:T(8,128)(2,1)}, u32[]{:S(2)}) copy-start(bf16[512,512]{1,0:T(8,128)(2,1)} %constant.8.clone.rh) | copy-start | bytes 1572868
  16.6 1.8 %copy-start.7 = (f32[1,256,256]{2,1,0:T(8,128)S(1)}, f32[1,256,256]{2,1,0:T(8,128)}, u32[]{:S(2)}) copy-start(f32[1,256,256]{2,1,0:T(8,128)} %param.10) | copy-start | bytes 786436
  16.6 18.5 %copy-start.6 = (bf16[512,512]{1,0:T(8,128)(2,1)S(1)}, bf16[512,512]{1,0:T(8,128)(2,1)}, u32[]{:S(2)}) copy-start(bf16[512,512]{1,0:T(8,128)(2,1)} %constant.8.clone.rh) | copy-start | bytes 1572868
  18.3 16.8 %copy-start.4 = (bf16[512,512]{1,0:T(8,128)(2,1)S(1)}, bf16[512,512]{1,0:T(8,128)(2,1)}, u32[]{:S(2)}) copy-start(bf16[512,512]{1,0:T(8,128)(2,1)} %constant.9.clone.rl) | copy-start | bytes 1572868

commit v4 on v3

--- a/solution.py
+++ b/solution.py
@@ -300,7 +300,13 @@
         rows[index] = piece.reshape(rounds, 2, block, width)
     share = square.shape[0]
     square[...] = power(probe_ref[pl.ds((scan * tiles + tile) * share, share)])
-    greet([(tile, tiles, tile_id), (mode, modes, mode_id)])
+    me = scan * tiles + tile
+    greet(
+        [
+            (me, scans * tiles, functools.partial(pattern_id, tiles)),
+            (scan + scans * mode, scans * modes, functools.partial(round_id, scans)),
+        ]
+    )
     copies = sends(tile, tiles, tile_id, lambda peer: rows.at[peer], got_ref, send, recv)
     copies += sends(mode, modes, mode_id, lambda peer: square, squares_ref, send_p, recv_p)
     got_ref[tile] = rows[tile]
@@ -327,9 +333,9 @@
     waves = times(probe_ref[...], window_ref[...])
     far = left_product(gh[...], gl[...], right_product(waves, rh[...], rl[...]))
     far_ref[...] = far
-    power_ref[...] = power(far)
+    power_ref[...] = power(far).reshape(power_ref.shape)
     square_ref[...] = jnp.sum(squares_ref[...], axis=0)
-    bright_ref[...] = power(window_ref[...])
+    bright_ref[...] = power(window_ref[...]).reshape(bright_ref.shape)
 
 
 def ratio_kernel(
@@ -340,7 +346,6 @@
     mode = lax.axis_index("mode")
     me = lax.axis_index("scan") * tiles + lax.axis_index("tile")
     id_of = functools.partial(pattern_id, tiles)
-    greet([(mode, modes, mode_id), (me, scans * tiles, id_of)])
     first = sends(mode, modes, mode_id, lambda peer: power_ref.at[peer], got, send, recv)
     other = sends(me, scans * tiles, id_of, lambda peer: square_ref, squares_ref, send_p, recv_p)
     more = sends(
@@ -367,7 +372,7 @@
 
 def inverse_kernel(
     sizes, places_ref, ratio_ref, far_ref, window_ref, probe_ref, rh, rl, gh, gl,
-    terms_ref, mixed_ref,
+    terms_ref, mixed_ref, ordered,
 ):
     width = probe_ref.shape[0]
     block = terms_ref.shape[2]
@@ -375,16 +380,18 @@
     count = sizes[0] * tiles
     me = lax.axis_index("scan") * tiles + lax.axis_index("tile")
     start, _ = place_of(places_ref, me, block)
-    ratio = ratio_ref[...]
+    ratio = ratio_ref[...].reshape(width, width)
     scaled = far_ref[...] * jnp.concatenate([ratio, ratio], 1)
     waves = left_product(rh[...], rl[...], right_product(scaled, gh[...], gl[...]))
     probe, window = probe_ref[...], window_ref[...]
     difference = waves - times(probe, window)
     terms = conj_times(probe, difference)
-    for index in range(width // block):
-        owner = lax.rem(start + index, count)
-        terms_ref[owner, index // count] = terms[index * block : (index + 1) * block]
-    mixed_ref[...] = conj_times(window, difference)
+    ordered[...] = terms.reshape(ordered.shape)
+    for owner in range(count):
+        first = lax.rem(owner - start + count * block * block, count)
+        for index in range(terms_ref.shape[1]):
+            terms_ref[owner, index] = ordered[first + count * index]
+    mixed_ref[...] = conj_times(window, difference).reshape(mixed_ref.shape)
 
 
 def reduce_kernel(
@@ -398,12 +405,12 @@
     rounds, block, width2 = terms_ref.shape[1:]
     width = width2 // 2
     columns = object_ref.shape[-1]
+    share = got_p.shape[1]
     scan, tile, mode = lax.axis_index("scan"), lax.axis_index("tile"), lax.axis_index("mode")
     me = scan * tiles + tile
     cycle = scan + scans * mode
     id_of = functools.partial(pattern_id, tiles)
     id_round = functools.partial(round_id, scans)
-    greet([(me, count, id_of), (cycle, scans * modes, id_round)])
     moves_t = sends(me, count, id_of, lambda peer: terms_ref.at[peer], got_t, send_t, recv_t)
     got_t[me] = terms_ref[me]
     got_p[me] = mixed_ref[me]
@@ -452,42 +459,46 @@
     for index in range(1, count):
         totals = totals + got_p[index]
     divisor = bright_ref[...]
-    next_ref[me] = probe_ref[me] + totals / jnp.concatenate([divisor, divisor], 1)
+    next_ref[me] = probe_ref[pl.ds(me * share, share)] + totals / jnp.concatenate([divisor, divisor], 1)
     last += sends(me, count, id_of, lambda peer: next_ref.at[me], next_ref, send_n, recv_n)
     for copy in last:
         copy.wait()
 
 
+def wave_kernel(
+    sizes, places_ref, object_ref, probe_ref, measured_ref, rh, rl, gh, gl, out_ref, next_ref,
+    rows, square, got_w, squares_m, window, far, strength, square_m, bright,
+    ratio, squares, bright_sum, got_s, got_b, terms, mixed, ordered, squares_b,
+    got_t, got_p, canvas, got_c, *sems,
+):
+    fetch_kernel(
+        sizes, places_ref, object_ref, probe_ref, got_w, squares_m, rows, square, *sems[:4]
+    )
+    forward_kernel(
+        sizes, places_ref, got_w, squares_m, probe_ref, rh, rl, gh, gl,
+        window, far, strength, square_m, bright,
+    )
+    ratio_kernel(
+        sizes, strength, square_m, bright, measured_ref, ratio, squares, bright_sum,
+        got_s, got_b, *sems[4:12],
+    )
+    inverse_kernel(
+        sizes, places_ref, ratio, far, window, probe_ref, rh, rl, gh, gl,
+        terms, mixed, ordered,
+    )
+    squares_b[...] = squares[...].reshape(squares_b.shape)
+    reduce_kernel(
+        sizes, places_ref, terms, mixed, probe_ref, squares_b, bright_sum, object_ref,
+        out_ref, next_ref, got_t, got_p, canvas, got_c, *sems[12:],
+    )
+
+
 def shape(*dims):
     return jax.ShapeDtypeStruct(dims, f32)
 
 
 def dma(count):
     return pltpu.SemaphoreType.DMA((count,))
-
-
-def local(kernel, in_specs, outs, scratch=()):
-    return pl.pallas_call(
-        kernel,
-        out_shape=outs,
-        in_specs=in_specs,
-        out_specs=jax.tree.map(lambda _: VMEM, outs),
-        scratch_shapes=list(scratch),
-        compiler_params=pltpu.CompilerParams(vmem_limit_bytes=vmem_bytes),
-    )
-
-
-def remote(kernel, number, inputs, outs, scratch):
-    return pl.pallas_call(
-        kernel,
-        out_shape=outs,
-        in_specs=inputs,
-        out_specs=[VMEM] * len(outs),
-        scratch_shapes=scratch,
-        compiler_params=pltpu.CompilerParams(
-            collective_id=number, has_side_effects=True, vmem_limit_bytes=vmem_bytes
-        ),
-    )
 
 
 def one_wave(sizes, tables, object_field, probe_modes, intensities, positions):
@@ -497,77 +508,51 @@
     cycles, _, block, _, columns = object_field.shape
     blocks = width // block
     rounds = blocks // tiles
+    parts = blocks // count
     share = width // count
     quarter = width // modes
-    places = positions.T
-    probe = probe_modes[0]
     planar = jnp.swapaxes(object_field[:, 0], 1, 2)
-    got, squares = remote(
-        functools.partial(fetch_kernel, sizes),
-        0,
-        [SMEM, VMEM, VMEM],
-        [shape(tiles, rounds, 2, block, width), shape(modes, share, width)],
-        [
-            pltpu.VMEM((tiles, rounds, 2, block, width), f32),
-            pltpu.VMEM((share, width), f32),
-        ]
-        + [dma(tiles - 1)] * 2
-        + [dma(modes - 1)] * 2,
-    )(places, planar, probe)
-    window, far, strength, square, bright = local(
-        functools.partial(forward_kernel, sizes),
-        [SMEM] + [VMEM] * 7,
-        [
-            shape(width, 2 * width),
-            shape(width, 2 * width),
-            shape(width, width),
-            shape(share, width),
-            shape(width, width),
-        ],
-    )(places, got, squares, probe, *tables)
-    ratio, squares, bright = remote(
-        functools.partial(ratio_kernel, sizes),
-        1,
-        [VMEM] * 4,
-        [shape(modes, quarter, width), shape(count, share, width), shape(share, width)],
-        [pltpu.VMEM((modes, quarter, width), f32), pltpu.VMEM((count, share, width), f32)]
-        + [dma(modes - 1)] * 4
-        + [dma(count - 1)] * 4,
+    buffers = [
+        (tiles, rounds, 2, block, width),
+        (share, width),
+        (tiles, rounds, 2, block, width),
+        (modes, share, width),
+        (width, 2 * width),
+        (width, 2 * width),
+        (modes, quarter, width),
+        (share, width),
+        (count, share, width),
+        (modes, quarter, width),
+        (count, share, width),
+        (share, width),
+        (modes, quarter, width),
+        (count, share, width),
+        (count, parts, block, 2 * width),
+        (count, share, 2 * width),
+        (blocks, block, 2 * width),
+        (blocks, block, width),
+        (count, parts, block, 2 * width),
+        (count, share, 2 * width),
+        (modes, 2, block, columns),
+        (modes, 2, block, columns),
+    ]
+    peers = [tiles] * 2 + [modes] * 6 + [count] * 8 + [modes] * 2 + [cycles] * 2 + [count] * 2
+    updated, probe_next = pl.pallas_call(
+        functools.partial(wave_kernel, sizes),
+        out_shape=[shape(cycles, 2, block, columns), shape(count, share, 2 * width)],
+        in_specs=[SMEM] + [VMEM] * 7,
+        out_specs=[VMEM] * 2,
+        scratch_shapes=[pltpu.VMEM(dims, f32) for dims in buffers]
+        + [dma(peer - 1) for peer in peers],
+        compiler_params=pltpu.CompilerParams(
+            collective_id=0, has_side_effects=True, vmem_limit_bytes=vmem_bytes
+        ),
     )(
-        strength.reshape(modes, quarter, width),
-        square,
-        bright.reshape(count, share, width),
+        positions.T,
+        planar,
+        probe_modes[0],
         intensities.reshape(modes, quarter, width),
-    )
-    parts = blocks // count
-    terms, mixed = local(
-        functools.partial(inverse_kernel, sizes),
-        [SMEM] + [VMEM] * 8,
-        [shape(count, parts, block, 2 * width), shape(width, 2 * width)],
-    )(places, ratio.reshape(width, width), far, window, probe, *tables)
-    updated, probe_next = remote(
-        functools.partial(reduce_kernel, sizes),
-        2,
-        [SMEM] + [VMEM] * 6,
-        [shape(cycles, 2, block, columns), shape(count, share, 2 * width)],
-        [
-            pltpu.VMEM((count, parts, block, 2 * width), f32),
-            pltpu.VMEM((count, share, 2 * width), f32),
-            pltpu.VMEM((modes, 2, block, columns), f32),
-            pltpu.VMEM((modes, 2, block, columns), f32),
-        ]
-        + [dma(count - 1)] * 4
-        + [dma(modes - 1)] * 2
-        + [dma(cycles - 1)] * 2
-        + [dma(count - 1)] * 2,
-    )(
-        places,
-        terms,
-        mixed.reshape(count, share, 2 * width),
-        probe.reshape(count, share, 2 * width),
-        squares.reshape(blocks, block, width),
-        bright,
-        planar,
+        *tables,
     )
     new_object = jnp.swapaxes(updated, 1, 2)[:, None]
     return (new_object, probe_next.reshape(1, width, 2 * width))

time: 67.1 us -> 63.1 us (0.940)
  Pallas kernels: 60.1 us -> 54.1 us
  local copies, waits for them, and re-layouts: 5.7 us -> 7.7 us
    pallas_call x5 -> x1, Pallas kernels: 60.1 us -> 54.1 us  [one_wave(): pl.pallas_call(functools.partial(wave_kernel, sizes), out_shape=[shape(cy...]
    unnamed x21 -> x17, local copies, waits for them, and re-layouts: 5.7 us -> 7.7 us
where the time goes in v4:
time: 63.1 us; the launch traced here: 62.4 us
  Pallas kernels  54.1 us (86%)
  local copies, waits for them, and re-layouts  7.7 us (12%)
  between operations  0.67 us (1%)
    pallas_call x1, Pallas kernels, one_wave(): pl.pallas_call(functools.partial(wave_kernel, sizes), out_shape=[shape(cy...  54.1 us
    unnamed x17, local copies, waits for them, and re-layouts  7.7 us

profile of v4, /device:TPU:0, one launch (start us, length us, event | category | flops | bytes accessed | tf_op | source)
XLA Modules:
  0.0 62.4 jit_solution(8041383006749543510)
XLA Ops:
  0.6 0.0 copy-start
  0.6 0.0 copy-start.5
  0.6 1.1 %copy.13 = f32[8,1,16,2,384]{4,2,3,0,1:T(8,128)S(1)} copy(f32[8,1,16,2,384]{4,3,2,1,0:T(2,128)} %param.8) | data formatting | bytes 786432 | tf_op args[0]
  1.7 0.0 copy-start.6
  1.8 0.0 copy-done
  1.8 0.1 copy-done.5
  1.9 0.6 copy-done.6
  2.5 0.0 copy-start.1
  2.5 1.0 %copy-done.1 = bf16[512,512]{1,0:T(8,128)(2,1)S(1)} copy-done((bf16[512,512]{1,0:T(8,128)(2,1)S(1)}, bf16[512,512]{1,0:T(8,128)(2,1)}, u32[]{:S(2)}) %copy-start.1) | copy-done | bytes 524312
  3.5 0.0 copy-start.2
  3.5 1.0 %copy-done.2 = bf16[512,512]{1,0:T(8,128)(2,1)S(1)} copy-done((bf16[512,512]{1,0:T(8,128)(2,1)S(1)}, bf16[512,512]{1,0:T(8,128)(2,1)}, u32[]{:S(2)}) %copy-start.2) | copy-done | bytes 524312
  4.5 0.0 copy-start.3
  4.5 1.0 %copy-done.3 = bf16[512,512]{1,0:T(8,128)(2,1)S(1)} copy-done((bf16[512,512]{1,0:T(8,128)(2,1)S(1)}, bf16[512,512]{1,0:T(8,128)(2,1)}, u32[]{:S(2)}) %copy-start.3) | copy-done | bytes 524312
  5.6 0.0 copy-start.4
  5.6 1.0 %copy-done.4 = bf16[512,512]{1,0:T(8,128)(2,1)S(1)} copy-done((bf16[512,512]{1,0:T(8,128)(2,1)S(1)}, bf16[512,512]{1,0:T(8,128)(2,1)}, u32[]{:S(2)}) %copy-start.4) | copy-done | bytes 524312
  6.6 54.1 %shard_map.95 = (f32[8,2,16,384]{3,2,1,0:T(8,128)S(1)}, f32[8,32,512]{2,1,0:T(8,128)S(1)}) custom-call(s32[2,8]{1,0:T(2,128)S(1)} %bitcast.17, f32[8,2,16,384]{3,2,1,0:T(8,128)S(1)} %bitcast.12, f32[256,512]{1,0:T(8,128)S(1)} %bitcast.14, f32[4,64,256]{2,1,0:T(8,128)S(1)} %bitcast.16, bf16[512,512]{1,0:T(8,128)(2,1)S(1)} %copy-done.4, ...), custom_call_target="tpu_custom_call" | custom-call | tf_op jit(solution)/shard_map/pallas_call | solution.py:540
  60.7 0.9 %copy.11 = f32[8,1,16,2,384]{4,3,2,1,0:T(2,128)} copy(f32[8,1,16,2,384]{4,2,3,0,1:T(8,128)S(1)} %bitcast.15) | data formatting | bytes 786432
  61.6 0.8 %copy.15 = f32[1,256,512]{2,1,0:T(8,128)} copy(f32[1,256,512]{2,1,0:T(8,128)S(1)} %bitcast.13) | data formatting | bytes 1048576
Async XLA Ops:
  0.6 1.2 %copy-start = (f32[1,256,512]{2,1,0:T(8,128)S(1)}, f32[1,256,512]{2,1,0:T(8,128)}, u32[]{:S(2)}) copy-start(f32[1,256,512]{2,1,0:T(8,128)} %param.9) | copy-start | bytes 1572868
  0.6 1.2 %copy-start.5 = (f32[1,256,256]{2,1,0:T(8,128)S(1)}, f32[1,256,256]{2,1,0:T(8,128)}, u32[]{:S(2)}) copy-start(f32[1,256,256]{2,1,0:T(8,128)} %param.10) | copy-start | bytes 786436
  1.7 0.7 %copy-start.6 = (s32[8,2]{0,1:T(2,128)S(1)}, s32[8,2]{0,1:T(2,128)}, u32[]{:S(2)}) copy-start(s32[8,2]{0,1:T(2,128)} %param.11) | copy-start | bytes 196
  2.5 1.0 %copy-start.1 = (bf16[512,512]{1,0:T(8,128)(2,1)S(1)}, bf16[512,512]{1,0:T(8,128)(2,1)}, u32[]{:S(2)}) copy-start(bf16[512,512]{1,0:T(8,128)(2,1)} %constant.11.clone.gl) | copy-start | bytes 1572868
  3.5 1.0 %copy-start.2 = (bf16[512,512]{1,0:T(8,128)(2,1)S(1)}, bf16[512,512]{1,0:T(8,128)(2,1)}, u32[]{:S(2)}) copy-start(bf16[512,512]{1,0:T(8,128)(2,1)} %constant.10.clone.gh) | copy-start | bytes 1572868
  4.5 1.0 %copy-start.3 = (bf16[512,512]{1,0:T(8,128)(2,1)S(1)}, bf16[512,512]{1,0:T(8,128)(2,1)}, u32[]{:S(2)}) copy-start(bf16[512,512]{1,0:T(8,128)(2,1)} %constant.9.clone.rl) | copy-start | bytes 1572868
  5.6 1.0 %copy-start.4 = (bf16[512,512]{1,0:T(8,128)(2,1)S(1)}, bf16[512,512]{1,0:T(8,128)(2,1)}, u32[]{:S(2)}) copy-start(bf16[512,512]{1,0:T(8,128)(2,1)} %constant.8.clone.rh) | copy-start | bytes 1572868

commit v5 on v4

--- a/solution.py
+++ b/solution.py
@@ -410,7 +410,6 @@
     me = scan * tiles + tile
     cycle = scan + scans * mode
     id_of = functools.partial(pattern_id, tiles)
-    id_round = functools.partial(round_id, scans)
     moves_t = sends(me, count, id_of, lambda peer: terms_ref.at[peer], got_t, send_t, recv_t)
     got_t[me] = terms_ref[me]
     got_p[me] = mixed_ref[me]
@@ -450,9 +449,35 @@
         for index in range(1, modes):
             total = total + got_c[index, part]
         out_ref[cycle, part] = object_ref[cycle, part] + total / (weight + damping)
-    last = sends(
-        cycle, scans * modes, id_round, lambda peer: out_ref.at[cycle], out_ref, send_o, recv_o
-    )
+
+    def pass_on(at, slot, target):
+        copy = pltpu.make_async_remote_copy(
+            src_ref=out_ref.at[at],
+            dst_ref=out_ref.at[at],
+            send_sem=send_o.at[slot],
+            recv_sem=recv_o.at[slot],
+            device_id=target,
+            device_id_type=MESH,
+        )
+        copy.start()
+        return copy
+
+    def across(step):
+        at = scan + scans * lax.rem(mode - step + modes, modes)
+        return [
+            pass_on(
+                at,
+                modes - 1 + step * (scans - 1) + turn - 1,
+                {"scan": lax.rem(scan + turn, scans)},
+            )
+            for turn in range(1, scans)
+        ]
+
+    along = [
+        pass_on(cycle, step - 1, mode_id(lax.rem(mode + step, modes)))
+        for step in range(1, modes)
+    ]
+    last = across(0)
     for copy in moves_p:
         copy.wait()
     totals = got_p[0]
@@ -461,6 +486,11 @@
     divisor = bright_ref[...]
     next_ref[me] = probe_ref[pl.ds(me * share, share)] + totals / jnp.concatenate([divisor, divisor], 1)
     last += sends(me, count, id_of, lambda peer: next_ref.at[me], next_ref, send_n, recv_n)
+    for step in range(1, modes):
+        along[step - 1].wait_recv()
+        last += across(step)
+    for copy in along:
+        copy.wait_send()
     for copy in last:
         copy.wait()
 

time: 63.1 us -> 64.4 us (1.021)
  Pallas kernels: 54.1 us -> 55.7 us
    pallas_call x1, Pallas kernels: 54.1 us -> 55.7 us  [one_wave(): pl.pallas_call(functools.partial(wave_kernel, sizes), out_shape=[shape(cy...]
where the time goes in v5:
time: 64.4 us; the launch traced here: 64 us
  Pallas kernels  55.7 us (86%)
  local copies, waits for them, and re-layouts  7.7 us (12%)
  between operations  0.67 us (1%)
    pallas_call x1, Pallas kernels, one_wave(): pl.pallas_call(functools.partial(wave_kernel, sizes), out_shape=[shape(cy...  55.7 us
    unnamed x17, local copies, waits for them, and re-layouts  7.7 us

profile of v5, /device:TPU:0, one launch (start us, length us, event | category | flops | bytes accessed | tf_op | source)
XLA Modules:
  0.0 64.0 jit_solution(8782388816306016077)
XLA Ops:
  0.6 0.0 copy-start
  0.6 0.0 copy-start.5
  0.6 1.1 %copy.13 = f32[8,1,16,2,384]{4,2,3,0,1:T(8,128)S(1)} copy(f32[8,1,16,2,384]{4,3,2,1,0:T(2,128)} %param.8) | data formatting | bytes 786432 | tf_op args[0]
  1.7 0.0 copy-start.6
  1.8 0.0 copy-done
  1.8 0.1 copy-done.5
  1.9 0.6 copy-done.6
  2.5 0.0 copy-start.1
  2.5 1.0 %copy-done.1 = bf16[512,512]{1,0:T(8,128)(2,1)S(1)} copy-done((bf16[512,512]{1,0:T(8,128)(2,1)S(1)}, bf16[512,512]{1,0:T(8,128)(2,1)}, u32[]{:S(2)}) %copy-start.1) | copy-done | bytes 524312
  3.5 0.0 copy-start.2
  3.5 1.0 %copy-done.2 = bf16[512,512]{1,0:T(8,128)(2,1)S(1)} copy-done((bf16[512,512]{1,0:T(8,128)(2,1)S(1)}, bf16[512,512]{1,0:T(8,128)(2,1)}, u32[]{:S(2)}) %copy-start.2) | copy-done | bytes 524312
  4.5 0.0 copy-start.3
  4.5 1.0 %copy-done.3 = bf16[512,512]{1,0:T(8,128)(2,1)S(1)} copy-done((bf16[512,512]{1,0:T(8,128)(2,1)S(1)}, bf16[512,512]{1,0:T(8,128)(2,1)}, u32[]{:S(2)}) %copy-start.3) | copy-done | bytes 524312
  5.6 0.0 copy-start.4
  5.6 1.0 %copy-done.4 = bf16[512,512]{1,0:T(8,128)(2,1)S(1)} copy-done((bf16[512,512]{1,0:T(8,128)(2,1)S(1)}, bf16[512,512]{1,0:T(8,128)(2,1)}, u32[]{:S(2)}) %copy-start.4) | copy-done | bytes 524312
  6.6 55.7 %shard_map.95 = (f32[8,2,16,384]{3,2,1,0:T(8,128)S(1)}, f32[8,32,512]{2,1,0:T(8,128)S(1)}) custom-call(s32[2,8]{1,0:T(2,128)S(1)} %bitcast.17, f32[8,2,16,384]{3,2,1,0:T(8,128)S(1)} %bitcast.12, f32[256,512]{1,0:T(8,128)S(1)} %bitcast.14, f32[4,64,256]{2,1,0:T(8,128)S(1)} %bitcast.16, bf16[512,512]{1,0:T(8,128)(2,1)S(1)} %copy-done.4, ...), custom_call_target="tpu_custom_call" | custom-call | tf_op jit(solution)/shard_map/pallas_call | solution.py:570
  62.3 0.9 %copy.11 = f32[8,1,16,2,384]{4,3,2,1,0:T(2,128)} copy(f32[8,1,16,2,384]{4,2,3,0,1:T(8,128)S(1)} %bitcast.15) | data formatting | bytes 786432
  63.3 0.8 %copy.15 = f32[1,256,512]{2,1,0:T(8,128)} copy(f32[1,256,512]{2,1,0:T(8,128)S(1)} %bitcast.13) | data formatting | bytes 1048576
Async XLA Ops:
  0.6 1.2 %copy-start = (f32[1,256,512]{2,1,0:T(8,128)S(1)}, f32[1,256,512]{2,1,0:T(8,128)}, u32[]{:S(2)}) copy-start(f32[1,256,512]{2,1,0:T(8,128)} %param.9) | copy-start | bytes 1572868
  0.6 1.2 %copy-start.5 = (f32[1,256,256]{2,1,0:T(8,128)S(1)}, f32[1,256,256]{2,1,0:T(8,128)}, u32[]{:S(2)}) copy-start(f32[1,256,256]{2,1,0:T(8,128)} %param.10) | copy-start | bytes 786436
  1.7 0.7 %copy-start.6 = (s32[8,2]{0,1:T(2,128)S(1)}, s32[8,2]{0,1:T(2,128)}, u32[]{:S(2)}) copy-start(s32[8,2]{0,1:T(2,128)} %param.11) | copy-start | bytes 196
  2.5 1.0 %copy-start.1 = (bf16[512,512]{1,0:T(8,128)(2,1)S(1)}, bf16[512,512]{1,0:T(8,128)(2,1)}, u32[]{:S(2)}) copy-start(bf16[512,512]{1,0:T(8,128)(2,1)} %constant.11.clone.gl) | copy-start | bytes 1572868
  3.5 1.0 %copy-start.2 = (bf16[512,512]{1,0:T(8,128)(2,1)S(1)}, bf16[512,512]{1,0:T(8,128)(2,1)}, u32[]{:S(2)}) copy-start(bf16[512,512]{1,0:T(8,128)(2,1)} %constant.10.clone.gh) | copy-start | bytes 1572868
  4.5 1.0 %copy-start.3 = (bf16[512,512]{1,0:T(8,128)(2,1)S(1)}, bf16[512,512]{1,0:T(8,128)(2,1)}, u32[]{:S(2)}) copy-start(bf16[512,512]{1,0:T(8,128)(2,1)} %constant.9.clone.rl) | copy-start | bytes 1572868
  5.6 1.0 %copy-start.4 = (bf16[512,512]{1,0:T(8,128)(2,1)S(1)}, bf16[512,512]{1,0:T(8,128)(2,1)}, u32[]{:S(2)}) copy-start(bf16[512,512]{1,0:T(8,128)(2,1)} %constant.8.clone.rh) | copy-start | bytes 1572868

commit v6 on v4

--- a/solution.py
+++ b/solution.py
@@ -260,7 +260,7 @@
                 barrier, inc=1, device_id=id_of(lax.rem(me + step, count)), device_id_type=MESH
             )
             total += 1
-    pl.semaphore_wait(barrier, total)
+    return barrier, total
 
 
 def tile_id(peer):
@@ -289,6 +289,13 @@
 ):
     scans, tiles, modes = sizes
     scan, tile, mode = lax.axis_index("scan"), lax.axis_index("tile"), lax.axis_index("mode")
+    me = scan * tiles + tile
+    barrier, total = greet(
+        [
+            (me, scans * tiles, functools.partial(pattern_id, tiles)),
+            (scan + scans * mode, scans * modes, functools.partial(round_id, scans)),
+        ]
+    )
     block = object_ref.shape[2]
     columns = object_ref.shape[3]
     rounds, width = rows.shape[1], rows.shape[4]
@@ -300,13 +307,7 @@
         rows[index] = piece.reshape(rounds, 2, block, width)
     share = square.shape[0]
     square[...] = power(probe_ref[pl.ds((scan * tiles + tile) * share, share)])
-    me = scan * tiles + tile
-    greet(
-        [
-            (me, scans * tiles, functools.partial(pattern_id, tiles)),
-            (scan + scans * mode, scans * modes, functools.partial(round_id, scans)),
-        ]
-    )
+    pl.semaphore_wait(barrier, total)
     copies = sends(tile, tiles, tile_id, lambda peer: rows.at[peer], got_ref, send, recv)
     copies += sends(mode, modes, mode_id, lambda peer: square, squares_ref, send_p, recv_p)
     got_ref[tile] = rows[tile]
@@ -391,11 +392,12 @@
         first = lax.rem(owner - start + count * block * block, count)
         for index in range(terms_ref.shape[1]):
             terms_ref[owner, index] = ordered[first + count * index]
-    mixed_ref[...] = conj_times(window, difference).reshape(mixed_ref.shape)
+    mixed_ref[...] = difference.reshape(mixed_ref.shape)
 
 
 def reduce_kernel(
-    sizes, places_ref, terms_ref, mixed_ref, probe_ref, square_ref, bright_ref, object_ref,
+    sizes, places_ref, window_ref, squares_ref,
+    terms_ref, mixed_ref, probe_ref, square_ref, bright_ref, object_ref,
     out_ref, next_ref,
     got_t, got_p, canvas, got_c,
     send_t, recv_t, send_m, recv_m, send_c, recv_c, send_o, recv_o, send_n, recv_n,
@@ -413,6 +415,8 @@
     id_round = functools.partial(round_id, scans)
     moves_t = sends(me, count, id_of, lambda peer: terms_ref.at[peer], got_t, send_t, recv_t)
     got_t[me] = terms_ref[me]
+    square_ref[...] = squares_ref[...].reshape(square_ref.shape)
+    mixed_ref[...] = conj_times(window_ref[...].reshape(mixed_ref.shape), mixed_ref[...])
     got_p[me] = mixed_ref[me]
     blank = jnp.zeros((block, columns - width), f32)
     zero = jnp.zeros((block, columns), f32)
@@ -486,9 +490,8 @@
         sizes, places_ref, ratio, far, window, probe_ref, rh, rl, gh, gl,
         terms, mixed, ordered,
     )
-    squares_b[...] = squares[...].reshape(squares_b.shape)
     reduce_kernel(
-        sizes, places_ref, terms, mixed, probe_ref, squares_b, bright_sum, object_ref,
+        sizes, places_ref, window, squares, terms, mixed, probe_ref, squares_b, bright_sum, object_ref,
         out_ref, next_ref, got_t, got_p, canvas, got_c, *sems[12:],
     )
 

time: 63.1 us -> 62.7 us (level)
  no operation moved by 1% of the time
where the time goes in v6:
time: 62.7 us; the launch traced here: 62.1 us
  Pallas kernels  53.7 us (86%)
  local copies, waits for them, and re-layouts  7.7 us (12%)
  between operations  0.67 us (1%)
    pallas_call x1, Pallas kernels, one_wave(): pl.pallas_call(functools.partial(wave_kernel, sizes), out_shape=[shape(cy...  53.7 us
    unnamed x17, local copies, waits for them, and re-layouts  7.7 us

profile of v6, /device:TPU:0, one launch (start us, length us, event | category | flops | bytes accessed | tf_op | source)
XLA Modules:
  0.0 62.1 jit_solution(7013137341885701879)
XLA Ops:
  0.6 0.0 copy-start
  0.6 0.0 copy-start.5
  0.6 1.1 %copy.13 = f32[8,1,16,2,384]{4,2,3,0,1:T(8,128)S(1)} copy(f32[8,1,16,2,384]{4,3,2,1,0:T(2,128)} %param.8) | data formatting | bytes 786432 | tf_op args[0]
  1.7 0.0 copy-start.6
  1.8 0.0 copy-done
  1.8 0.1 copy-done.5
  1.9 0.6 copy-done.6
  2.5 0.0 copy-start.1
  2.5 1.0 %copy-done.1 = bf16[512,512]{1,0:T(8,128)(2,1)S(1)} copy-done((bf16[512,512]{1,0:T(8,128)(2,1)S(1)}, bf16[512,512]{1,0:T(8,128)(2,1)}, u32[]{:S(2)}) %copy-start.1) | copy-done | bytes 524312
  3.5 0.0 copy-start.2
  3.5 1.0 %copy-done.2 = bf16[512,512]{1,0:T(8,128)(2,1)S(1)} copy-done((bf16[512,512]{1,0:T(8,128)(2,1)S(1)}, bf16[512,512]{1,0:T(8,128)(2,1)}, u32[]{:S(2)}) %copy-start.2) | copy-done | bytes 524312
  4.5 0.0 copy-start.3
  4.5 1.0 %copy-done.3 = bf16[512,512]{1,0:T(8,128)(2,1)S(1)} copy-done((bf16[512,512]{1,0:T(8,128)(2,1)S(1)}, bf16[512,512]{1,0:T(8,128)(2,1)}, u32[]{:S(2)}) %copy-start.3) | copy-done | bytes 524312
  5.6 0.0 copy-start.4
  5.6 1.0 %copy-done.4 = bf16[512,512]{1,0:T(8,128)(2,1)S(1)} copy-done((bf16[512,512]{1,0:T(8,128)(2,1)S(1)}, bf16[512,512]{1,0:T(8,128)(2,1)}, u32[]{:S(2)}) %copy-start.4) | copy-done | bytes 524312
  6.6 53.7 %shard_map.95 = (f32[8,2,16,384]{3,2,1,0:T(8,128)S(1)}, f32[8,32,512]{2,1,0:T(8,128)S(1)}) custom-call(s32[2,8]{1,0:T(2,128)S(1)} %bitcast.17, f32[8,2,16,384]{3,2,1,0:T(8,128)S(1)} %bitcast.12, f32[256,512]{1,0:T(8,128)S(1)} %bitcast.14, f32[4,64,256]{2,1,0:T(8,128)S(1)} %bitcast.16, bf16[512,512]{1,0:T(8,128)(2,1)S(1)} %copy-done.4, ...), custom_call_target="tpu_custom_call" | custom-call | tf_op jit(solution)/shard_map/pallas_call | solution.py:543
  60.3 0.9 %copy.11 = f32[8,1,16,2,384]{4,3,2,1,0:T(2,128)} copy(f32[8,1,16,2,384]{4,2,3,0,1:T(8,128)S(1)} %bitcast.15) | data formatting | bytes 786432
  61.3 0.8 %copy.15 = f32[1,256,512]{2,1,0:T(8,128)} copy(f32[1,256,512]{2,1,0:T(8,128)S(1)} %bitcast.13) | data formatting | bytes 1048576
Async XLA Ops:
  0.6 1.2 %copy-start = (f32[1,256,512]{2,1,0:T(8,128)S(1)}, f32[1,256,512]{2,1,0:T(8,128)}, u32[]{:S(2)}) copy-start(f32[1,256,512]{2,1,0:T(8,128)} %param.9) | copy-start | bytes 1572868
  0.6 1.2 %copy-start.5 = (f32[1,256,256]{2,1,0:T(8,128)S(1)}, f32[1,256,256]{2,1,0:T(8,128)}, u32[]{:S(2)}) copy-start(f32[1,256,256]{2,1,0:T(8,128)} %param.10) | copy-start | bytes 786436
  1.7 0.7 %copy-start.6 = (s32[8,2]{0,1:T(2,128)S(1)}, s32[8,2]{0,1:T(2,128)}, u32[]{:S(2)}) copy-start(s32[8,2]{0,1:T(2,128)} %param.11) | copy-start | bytes 196
  2.5 1.0 %copy-start.1 = (bf16[512,512]{1,0:T(8,128)(2,1)S(1)}, bf16[512,512]{1,0:T(8,128)(2,1)}, u32[]{:S(2)}) copy-start(bf16[512,512]{1,0:T(8,128)(2,1)} %constant.11.clone.gl) | copy-start | bytes 1572868
  3.5 1.0 %copy-start.2 = (bf16[512,512]{1,0:T(8,128)(2,1)S(1)}, bf16[512,512]{1,0:T(8,128)(2,1)}, u32[]{:S(2)}) copy-start(bf16[512,512]{1,0:T(8,128)(2,1)} %constant.10.clone.gh) | copy-start | bytes 1572868
  4.5 1.0 %copy-start.3 = (bf16[512,512]{1,0:T(8,128)(2,1)S(1)}, bf16[512,512]{1,0:T(8,128)(2,1)}, u32[]{:S(2)}) copy-start(bf16[512,512]{1,0:T(8,128)(2,1)} %constant.9.clone.rl) | copy-start | bytes 1572868
  5.6 1.0 %copy-start.4 = (bf16[512,512]{1,0:T(8,128)(2,1)S(1)}, bf16[512,512]{1,0:T(8,128)(2,1)}, u32[]{:S(2)}) copy-start(bf16[512,512]{1,0:T(8,128)(2,1)} %constant.8.clone.rh) | copy-start | bytes 1572868
